TPU v7x, 32 devices: a whole 2x2x4 slice. The times are simulated.
32 devices in a mesh: fold: 4 (over x, core), blk: 8 (over z, y).
Axes of the slice: x: 2, y: 2, z: 4, core: 2. Of those that a mesh axis runs over, the one named last changes fastest.
Arguments:
- fine_rhs: float32 [1536, 32, 128], P(('fold', 'blk')), may hold values from -6 to 6
- fine_tiles: bfloat16 [1536, 5, 128, 128], P(('fold', 'blk')), as said below
- fine_cols: int32 [1536, 5], P(('fold', 'blk')), may hold values from 0 to 1535, as said below
- fine_smoother: bfloat16 [1536, 128, 128], P(('fold', 'blk'))
- fine_map: int32 [1536], P(('fold', 'blk')), may hold values from 0 to 383, as said below
- fine_slots: int32 [1536, 128], P(('fold', 'blk')), may hold values from 0 to 127
- mid_tiles: bfloat16 [384, 5, 128, 128], P(('fold', 'blk'))
- mid_cols: int32 [384, 5], P(('fold', 'blk')), may hold values from 0 to 383, as said below
- mid_smoother: bfloat16 [384, 128, 128], P(('fold', 'blk'))
- mid_map: int32 [384], P(('fold', 'blk')), may hold values from 0 to 95, as said below
- mid_slots: int32 [384, 128], P(('fold', 'blk')), may hold values from 0 to 127
- coarse_tiles: bfloat16 [96, 5, 128, 128], P('blk')
- coarse_cols: int32 [96, 5], P('blk'), may hold values from 0 to 95, as said below
- coarse_smoother: bfloat16 [96, 128, 128], P('blk')
Outputs:
- fine_field: float32 [1536, 32, 128], P(('fold', 'blk'))
- mid_field: float32 [384, 32, 128], P(('fold', 'blk'))
- coarse_field: float32 [96, 32, 128], P('blk')
Inputs may be any that keep to these rules, and one draw needn't show every extreme that they name: `fine_cols`: column 0 of each row names the row's own block; every other entry names a level-0 block of a device with the same fold index whose blk index differs by at most one, cyclically. `mid_cols`: column 0 of each row names the row's own block; every other entry names a level-1 block of a device with the same fold index whose blk index differs by at most one, cyclically. `coarse_cols`: column 0 of each row names the row's own block; every other entry names a level-2 block whose blk index differs from the row's by at most one, cyclically. `fine_map`: A level-0 block's level-1 block lies on a device with the same fold index; of the level-0 blocks of one device at most 12 have their level-1 blocks on any one device, and in every fold row some device receives exactly 12 from every device of that row. `mid_map`: A level-1 block's level-2 block lies at the same blk index. `fine_tiles`: each smoother tile is close to half the inverse of the diagonal of the row block's diagonal tile.
All inputs are finite; a program needn't handle non-finite values.
Results may differ from a plain program's by a relative error of at most 0.012.
Values may be sent and summed in bfloat16 or wider, within the bound.
No kernel may reach another device: no remote copies, remote signals or barrier semaphores. Data moves between devices by JAX's collectives and lax.ppermute only.
A program may use at most 128 MiB of HBM per device.

v0:
```python
import jax
import jax.numpy as jnp
from jax import lax
from jax.experimental import pallas as pl
from jax.experimental.pallas import tpu as pltpu
from jax.sharding import PartitionSpec as P

COARSE = 8
HALVES, CHUNKS = 2, 2
F32 = jnp.float32
BF16 = jnp.bfloat16
NT = (((1,), (1,)), ((), ()))
NN = (((1,), (0,)), ((), ()))
ANY = pl.BlockSpec(memory_space=pl.ANY)
VMEM = pl.BlockSpec(memory_space=pltpu.VMEM)
SMEM = pl.BlockSpec(memory_space=pltpu.SMEM)
MIB = 1 << 20


def sds(shape, dtype):
    return jax.ShapeDtypeStruct(shape, dtype)


def params(mib):
    return pltpu.CompilerParams(vmem_limit_bytes=mib * MIB)


def times(x, tile):
    return lax.dot_general(x, tile, NT, preferred_element_type=F32)


def first_before(per, folded):
    blks = lax.axis_size("blk")
    blk = lax.axis_index("blk")
    base = lax.axis_index("fold") * (blks * per) if folded else 0
    return base + (blk - 1) * per, blks * per


def picked(cols_ref, row, ring, x_ref):
    first, total = ring
    blocks = []
    for k in range(cols_ref.shape[0]):
        place = cols_ref[k, row] - first
        place = jnp.where(place < 0, place + total, place)
        place = jnp.where(place >= total, place - total, place)
        blocks.append(x_ref[place])
    return jnp.concatenate(blocks, axis=1).astype(BF16)


def row_product(cols_ref, row, ring, x_ref, tiles_ref):
    t = jnp.concatenate([tiles_ref[row, k] for k in range(tiles_ref.shape[1])], axis=1)
    return times(picked(cols_ref, row, ring, x_ref), t)


def packed_product(cols_ref, row, ring, x_ref, pack_ref):
    kt, vb = pack_ref.shape[1] - 1, pack_ref.shape[2]
    t = pack_ref[row, :kt].reshape(kt * vb, vb)
    x = picked(cols_ref, row, ring, x_ref)
    return lax.dot_general(x, t, NN, preferred_element_type=F32)


def smoothed(z, pack_ref, row):
    last = pack_ref.shape[1] - 1
    return lax.dot_general(z.astype(BF16), pack_ref[row, last], NN, preferred_element_type=F32)


def fill(dest, parts, at=0):
    for part in parts:
        dest[pl.ds(at, part.shape[0])] = part[...].astype(dest.dtype)
        at = at + part.shape[0]


def fill_pair(dest, parts, n):
    side = lax.axis_index("blk") % 2
    third = len(parts) // 3
    fill(dest, parts[:third], n)
    fill(dest, parts[third : 2 * third], (1 - side) * (2 * n))
    fill(dest, parts[2 * third :], side * (2 * n))


def in_groups(count):
    return next(g for g in (12, 8, 6, 4, 3, 2, 1) if count % g == 0)


def cost(us):
    return pl.CostEstimate(flops=0, bytes_accessed=int(us * 3.0e6), transcendentals=0)


def halos(value):
    n = lax.axis_size("blk")
    up = [(i, (i + 1) % n) for i in range(n)]
    down = [((i + 1) % n, i) for i in range(n)]
    return lax.ppermute(value, "blk", up), lax.ppermute(value, "blk", down)


def partner(value):
    n = lax.axis_size("blk")
    return lax.ppermute(value, "blk", [(i, i ^ 1) for i in range(n)])


def forwarded(value):
    n = lax.axis_size("blk")
    return lax.ppermute(value, "blk", [(i, (i + 2 - 4 * (i % 2)) % n) for i in range(n)])


def pair_halos(chunks):
    near = [partner(c) for c in chunks]
    return near + [forwarded(c) for c in near]


def store_chunks(i, value, h_refs):
    size = h_refs[0].shape[0]
    for c, h_ref in enumerate(h_refs):

        @pl.when((i >= c * size) & (i < (c + 1) * size))
        def _(c=c, h_ref=h_ref):
            h_ref[pl.ds(i - c * size, value.shape[0])] = value


def fine_first(low, count, chunks, smoother, rhs):
    n, r, vb = rhs.shape
    size = count // chunks
    g = in_groups(size)
    steps = count // g

    def kernel(m_ref, rhs_ref, f_ref, *h_refs):
        def step(j, carry):
            at = j * g
            vs = [
                times(rhs_ref[low + at + i].astype(BF16), m_ref[low + at + i]) for i in range(g)
            ]
            for i in range(g):
                f_ref[at + i] = vs[i]
            store_chunks(at, jnp.stack([v.astype(BF16) for v in vs]), h_refs)
            return carry

        lax.fori_loop(0, steps, step, 0)

    f, *h = pl.pallas_call(
        kernel,
        in_specs=[VMEM] * 2,
        out_specs=[VMEM] * (1 + chunks),
        out_shape=[sds((count, r, vb), F32)] + [sds((size, r, vb), BF16)] * chunks,
        compiler_params=params(12),
        cost_estimate=cost(count * 0.04),
    )(smoother, rhs)
    return f, h


def brought(source, after):
    n = source.shape[0]
    parts = in_groups(n)
    size = n // parts

    def kernel(source_ref, after_ref, copied_ref, sems):
        copies = []
        for p in range(parts):
            at = pl.ds(p * size, size)
            copies.append(pltpu.make_async_copy(source_ref.at[at], copied_ref.at[at], sems.at[p]))
        for copy in copies:
            copy.start()
        for copy in copies:
            copy.wait()

    return pl.pallas_call(
        kernel,
        in_specs=[ANY] * 2,
        out_specs=VMEM,
        out_shape=sds(source.shape, source.dtype),
        scratch_shapes=[pltpu.SemaphoreType.DMA((parts,))],
        compiler_params=params(12),
        cost_estimate=cost(3),
    )(source, after)


def fine_sweep(low, count, chunks, cols, x_parts, tiles, smoother, rhs, field):
    n, r, vb = rhs.shape
    size = count // chunks
    g = in_groups(size)
    steps = count // g
    parts = len(x_parts)

    def kernel(cols_ref, *refs):
        x_refs, (t_ref, m_ref, rhs_ref, v_ref, f_ref), (*h_refs, x_ref) = (
            refs[:parts],
            refs[parts : parts + 5],
            refs[parts + 5 :],
        )
        fill_pair(x_ref, x_refs, n)
        ring = first_before(n, True)

        def step(j, carry):
            at = j * g
            zs = []
            for i in range(g):
                row = low + at + i
                z = rhs_ref[row] - row_product(cols_ref, row, ring, x_ref, t_ref)
                zs.append(z.astype(BF16))
            vs = [v_ref[at + i] + times(zs[i], m_ref[low + at + i]) for i in range(g)]
            for i in range(g):
                f_ref[at + i] = vs[i]
            store_chunks(at, jnp.stack([v.astype(BF16) for v in vs]), h_refs)
            return carry

        lax.fori_loop(0, steps, step, 0)

    f, *h = pl.pallas_call(
        kernel,
        in_specs=[SMEM] + [VMEM] * (parts + 4),
        out_specs=[VMEM] * (1 + chunks),
        out_shape=[sds((count, r, vb), F32)] + [sds((size, r, vb), BF16)] * chunks,
        scratch_shapes=[pltpu.VMEM((3 * n, r, vb), BF16)],
        compiler_params=params(12),
        cost_estimate=cost(count * 0.15),
    )(cols, *x_parts, tiles, smoother, rhs, field)
    return f, h


def one_hot(slots_row, vb):
    return (lax.broadcasted_iota(jnp.int32, (vb, vb), 0) == slots_row).astype(F32).astype(BF16)


def collected(z, slots_row):
    r, vb = z.shape
    high = z.astype(BF16)
    low = (z - high.astype(F32)).astype(BF16)
    both = times(jnp.concatenate([high, low], axis=0), one_hot(slots_row, vb))
    return both[:r] + both[r:]


def fine_restrict(cols, to_mid, x_parts, pack, rhs, slots, map_row, n1):
    n, r, vb = rhs.shape
    g = in_groups(n)
    steps = n // g
    parts = len(x_parts)
    blks = lax.axis_size("blk")
    pairs = blks // 2
    half = pairs * n1
    map_rows = -(-n // vb)
    cut = (pairs + 1) // 2

    def kernel(cols_ref, to_ref, *refs):
        x_refs, refs = refs[:parts], refs[parts:]
        pack_ref, rhs_ref, s_ref, map_ref, z_ref, own_ref, *others, table_ref, x_ref, acc_ref = refs
        fill_pair(x_ref, x_refs, n)
        acc_ref[...] = jnp.zeros_like(acc_ref)
        table_ref[:n] = s_ref[...]
        for q in range(map_rows):
            size = min(vb, n - q * vb)
            table_ref[n + q : n + q + 1, :size] = map_ref[:, q * vb : q * vb + size]
        ring = first_before(n, True)
        side = lax.axis_index("blk") % 2
        base = lax.axis_index("fold") * (blks * n1)

        def step(j, carry):
            at = j * g
            zs = [
                rhs_ref[at + i] - packed_product(cols_ref, at + i, ring, x_ref, pack_ref)
                for i in range(g)
            ]
            for i in range(g):
                z_ref[at + i] = zs[i]
            pieces = [collected(zs[i], s_ref[pl.ds(at + i, 1), :]) for i in range(g)]
            for i in range(g):
                to = to_ref[at + i] - base
                blk = to // n1
                apart = jnp.where(blk % 2 == side, 0, half)
                acc_ref[apart + (blk // 2) * n1 + (to - blk * n1)] += pieces[i]
            return carry

        lax.fori_loop(0, steps, step, 0)
        own_ref[...] = acc_ref[:half]
        pair = lax.axis_index("blk") // 2
        for q in range(pairs):
            at = pl.ds(half + (pair + pairs - 1 - q) % pairs * n1, n1)
            place = q % cut * n1
            others[q // cut][place : place + n1] = acc_ref[at].astype(BF16)

    return pl.pallas_call(
        kernel,
        in_specs=[SMEM] * 2 + [VMEM] * (parts + 4),
        out_specs=[VMEM] * 5,
        out_shape=[
            sds(rhs.shape, F32),
            sds((half, r, vb), F32),
            sds((cut * n1, r, vb), BF16),
            sds(((pairs - cut) * n1, r, vb), BF16),
            sds((n + map_rows, vb), jnp.int32),
        ],
        scratch_shapes=[pltpu.VMEM((3 * n, r, vb), BF16), pltpu.VMEM((2 * half, r, vb), F32)],
        compiler_params=params(16),
        cost_estimate=cost(n * 0.15),
    )(cols, to_mid, *x_parts, pack, rhs, slots, map_row)


def pair_sums(own, got, last, n1):
    half, r, vb = own.shape
    count = got.shape[0] // n1

    def kernel(own_ref, got_ref, *refs):
        pair = lax.axis_index("blk") // 2
        for k in range(count):
            at = pl.ds((pair + last - k) % (half // n1) * n1, n1)
            total = own_ref[at] + got_ref[k * n1 : (k + 1) * n1].astype(F32)
            refs[k][...] = total.astype(BF16)

    return pl.pallas_call(
        kernel,
        in_specs=[VMEM] * 2,
        out_specs=[VMEM] * count,
        out_shape=[sds((n1, r, vb), BF16)] * count,
        compiler_params=params(12),
        cost_estimate=cost(0.2),
    )(own, got)


def fine_last(cols, to_mid, slots, tables, mid_parts, pack, resid, fields, others):
    n, r, vb = resid.shape
    g = in_groups(fields[0].shape[0])
    steps = n // g
    wide = next(w for w in (16, 12, 8, 6, 4, 3, 2, 1) if n % w == 0)
    parts = len(mid_parts)
    half = parts // 2
    n1 = mid_parts[0].shape[0]

    def kernel(cols_ref, to_ref, near_to_ref, far_to_ref, s_ref, near_ref, far_ref, *refs):
        mid_refs, (pack_ref, z_ref), refs = refs[:parts], refs[parts : parts + 2], refs[parts + 2 :]
        v_refs, refs = refs[: len(fields)], refs[len(fields) :]
        other_refs, (out_hbm, *other_hbm), (f_ref, x_ref, all_ref, sems, other_sems) = (
            refs[: len(others)],
            refs[len(others) : 2 * len(others) + 1],
            refs[2 * len(others) + 1 :],
        )
        other_copies = [
            pltpu.make_async_copy(source, dest, other_sems.at[q])
            for q, (source, dest) in enumerate(zip(other_refs, other_hbm))
        ]
        for copy in other_copies:
            copy.start()

        def out_copy(j):
            at = pl.ds(j * g, g)
            return pltpu.make_async_copy(f_ref.at[at], out_hbm.at[at], sems.at[j])

        blk = lax.axis_index("blk")
        side = blk % 2
        base = lax.axis_index("fold") * (parts * n1)
        for p in range(parts):
            owner = (blk // 2 + half - p % half) % half * 2 + (side if p < half else 1 - side)
            all_ref[pl.ds(owner * n1, n1)] = mid_refs[parts - 1 - p][...].astype(F32)

        def lift(start, slots_of, to_of):
            def some(j, carry):
                lifted = []
                for q in range(wide):
                    index = jnp.broadcast_to(slots_of[pl.ds(j * wide + q, 1), :], (r, vb))
                    h = all_ref[to_of(j * wide + q) - base]
                    lifted.append(jnp.take_along_axis(h, index, axis=1))
                for q in range(wide):
                    x_ref[start + j * wide + q] = lifted[q].astype(BF16)
                return carry

            lax.fori_loop(0, n // wide, some, 0)

        def from_table(ref):
            if n <= vb:
                return lambda i: ref[n, i]
            return lambda i: ref[n + i // vb, i % vb]

        lift(n, s_ref, lambda i: to_ref[i])
        lift((1 - side) * (2 * n), near_ref, from_table(near_to_ref))
        lift(side * (2 * n), far_ref, from_table(far_to_ref))
        ring = first_before(n, True)

        def step(j, v_ref, low):
            at = j * g
            zs = [
                z_ref[at + i] - packed_product(cols_ref, at + i, ring, x_ref, pack_ref)
                for i in range(g)
            ]
            vs = [smoothed(zs[i], pack_ref, at + i) for i in range(g)]
            for i in range(g):
                f_ref[at + i] = vs[i] + (v_ref[at - low + i] + x_ref[n + at + i].astype(F32))
            out_copy(j).start()

        low = 0
        for v_ref in v_refs:
            high = low + v_ref.shape[0]

            def some_rows(j, carry, v_ref=v_ref, low=low):
                step(j, v_ref, low)
                return carry

            lax.fori_loop(low // g, high // g, some_rows, 0)
            low = high
        for j in range(steps):
            out_copy(j).wait()
        for copy in other_copies:
            copy.wait()

    return pl.pallas_call(
        kernel,
        in_specs=[SMEM] * 4 + [VMEM] * (5 + parts + len(fields) + len(others)),
        out_specs=[ANY] * (1 + len(others)),
        out_shape=[sds(resid.shape, F32)] + [sds(a.shape, a.dtype) for a in others],
        scratch_shapes=[
            pltpu.VMEM((n, r, vb), F32),
            pltpu.VMEM((3 * n, r, vb), BF16),
            pltpu.VMEM((parts * n1, r, vb), F32),
            pltpu.SemaphoreType.DMA((steps,)),
            pltpu.SemaphoreType.DMA((len(others),)),
        ],
        compiler_params=params(16),
        cost_estimate=cost(n * 0.2),
    )(
        cols,
        to_mid,
        *tables,
        slots,
        *tables,
        *mid_parts[::-1],
        pack,
        resid,
        *fields,
        *others,
    )


def packed(tiles, smoother, after):
    n, kt, vb, _ = tiles.shape

    def kernel(t_ref, m_ref, after_ref, o_ref):
        def one(i, carry):
            for k in range(kt):
                o_ref[i, k] = t_ref[i, k].T
            o_ref[i, kt] = m_ref[i].T
            return carry

        lax.fori_loop(0, n, one, 0)

    return pl.pallas_call(
        kernel,
        in_specs=[VMEM] * 2 + [ANY],
        out_specs=VMEM,
        out_shape=sds((n, kt + 1, vb, vb), BF16),
        compiler_params=params(12),
        cost_estimate=cost(2),
    )(tiles, smoother, after)


def add_and_smooth(pack, terms):
    shape = terms[0].shape

    def kernel(pack_ref, *refs):
        term_refs, (rhs_ref, f_ref, h_ref) = refs[:-3], refs[-3:]
        totals = []
        for i in range(shape[0]):
            total = term_refs[0][i].astype(F32)
            for t in term_refs[1:]:
                total = total + t[i].astype(F32)
            totals.append(total)
        vs = [smoothed(total, pack_ref, i) for i, total in enumerate(totals)]
        for i, v in enumerate(vs):
            rhs_ref[i] = totals[i]
            f_ref[i] = v
            h_ref[i] = v.astype(BF16)

    return pl.pallas_call(
        kernel,
        in_specs=[VMEM] * (1 + len(terms)),
        out_specs=[VMEM] * 3,
        out_shape=[sds(shape, F32), sds(shape, F32), sds(shape, BF16)],
        compiler_params=params(12),
        cost_estimate=cost(0.3),
    )(pack, *terms)


def small_sweep(folded, cols, x3, pack, rhs, field, last=False):
    n, r, vb = rhs.shape
    pick = BF16 if r % 16 == 0 else F32
    kinds = [BF16] if last else [BF16, F32]

    def kernel(cols_ref, c_ref, b_ref, a_ref, pack_ref, rhs_ref, v_ref, *refs):
        out_refs, x_ref = refs[:-1], refs[-1]
        fill(x_ref, (a_ref, b_ref, c_ref))
        ring = first_before(n, folded)
        zs = [rhs_ref[i] - packed_product(cols_ref, i, ring, x_ref, pack_ref) for i in range(n)]
        vs = [v_ref[i] + smoothed(zs[i], pack_ref, i) for i in range(n)]
        for i, v in enumerate(vs):
            for out_ref in out_refs:
                out_ref[i] = v.astype(out_ref.dtype)

    return pl.pallas_call(
        kernel,
        in_specs=[SMEM] + [VMEM] * 6,
        out_specs=[VMEM] * len(kinds),
        out_shape=[sds(rhs.shape, kind) for kind in kinds],
        scratch_shapes=[pltpu.VMEM((3 * n, r, vb), pick)],
        compiler_params=params(12),
        cost_estimate=cost(1),
    )(cols, *x3[::-1], pack, rhs, field)


def mid_restrict(cols, to_low, x3, pack, rhs, slots, lows):
    n, r, vb = rhs.shape
    folds = lax.axis_size("fold")
    share = r // folds

    def kernel(cols_ref, to_ref, c_ref, b_ref, a_ref, pack_ref, rhs_ref, s_ref, *refs):
        outs, (x_ref, acc_ref, cut_ref) = refs[:folds], refs[folds:]
        fill(x_ref, (a_ref, b_ref, c_ref))
        acc_ref[...] = jnp.zeros_like(acc_ref)
        ring = first_before(n, True)
        zs = [rhs_ref[i] - packed_product(cols_ref, i, ring, x_ref, pack_ref) for i in range(n)]
        pieces = [collected(zs[i], s_ref[i : i + 1, :]) for i in range(n)]
        base = lax.axis_index("blk") * lows
        for i in range(n):
            acc_ref[to_ref[i] - base] += pieces[i]
        for f in range(folds):
            cut_ref[f] = acc_ref[:, f * share : (f + 1) * share, :]
        for f in range(folds):
            outs[f][...] = cut_ref[(lax.axis_index("fold") + f) % folds].astype(BF16)

    return pl.pallas_call(
        kernel,
        in_specs=[SMEM] * 2 + [VMEM] * 6,
        out_specs=[VMEM] * folds,
        out_shape=[sds((lows, share, vb), BF16)] * folds,
        scratch_shapes=[
            pltpu.VMEM((3 * n, r, vb), BF16),
            pltpu.VMEM((lows, r, vb), F32),
            pltpu.VMEM((folds, lows, share, vb), F32),
        ],
        compiler_params=params(12),
    )(cols, to_low, *x3[::-1], pack, rhs, slots)


def mid_lift(to_low, parts, field, slots):
    n, r, vb = field.shape
    folds = len(parts)
    lows, share = parts[0].shape[:2]

    def kernel(to_ref, *refs):
        part_refs, (v_ref, s_ref, c_ref, f_ref, h_ref, cut_ref) = refs[:folds], refs[folds:]
        for f in range(folds):
            owner = (lax.axis_index("fold") + folds - f) % folds
            cut_ref[owner] = part_refs[f][...].astype(F32)
        for f in range(folds):
            c_ref[:, f * share : (f + 1) * share, :] = cut_ref[f]
        for i in range(n):
            index = jnp.broadcast_to(s_ref[i : i + 1, :], (r, vb))
            low = to_ref[i] - lax.axis_index("blk") * lows
            v = v_ref[i] + jnp.take_along_axis(c_ref[low], index, axis=1)
            f_ref[i] = v
            h_ref[i] = v.astype(BF16)

    return pl.pallas_call(
        kernel,
        in_specs=[SMEM] + [VMEM] * (folds + 2),
        out_specs=[VMEM] * 3,
        out_shape=[sds((lows, r, vb), F32), sds(field.shape, F32), sds(field.shape, BF16)],
        scratch_shapes=[pltpu.VMEM((folds, lows, share, vb), F32)],
        compiler_params=params(16),
    )(to_low, *parts, field, slots)


def on_device(
    fine_rhs,
    fine_tiles,
    fine_cols,
    fine_smoother,
    fine_map,
    fine_slots,
    mid_tiles,
    mid_cols,
    mid_smoother,
    mid_map,
    mid_slots,
    coarse_tiles,
    coarse_cols,
    coarse_smoother,
):
    n0, r, vb = fine_rhs.shape
    n1 = mid_tiles.shape[0]
    n2 = coarse_tiles.shape[0]
    blks, folds = lax.axis_size("blk"), lax.axis_size("fold")
    pairs = blks // 2
    cols0, cols1, cols2 = fine_cols.T, mid_cols.T, coarse_cols.T

    halves, chunks = HALVES, CHUNKS
    count = n0 // halves
    v, h = [], []
    for k in range(halves):
        part, rough = fine_first(k * count, count, chunks, fine_smoother, fine_rhs)
        v.append(part)
        h += rough
    x = h + pair_halos(h)
    fine_tiles = brought(fine_tiles, x[2 * halves * chunks])
    down, h = [], []
    for k in range(halves):
        part, rough = fine_sweep(
            k * count, count, chunks, cols0, x, fine_tiles, fine_smoother, fine_rhs, v[k]
        )
        down.append(part)
        h += rough
    x = h + pair_halos(h)
    fine_pack = packed(fine_tiles, fine_smoother, x[2 * halves * chunks - 1])
    resid, own, *others, table = fine_restrict(
        cols0, fine_map, x, fine_pack, fine_rhs, fine_slots, fine_map[None], n1
    )
    steps = [[(i, (i + 2 * k) % blks) for i in range(blks)] for k in range(pairs)]
    late = partner(others[1])
    early = partner(others[0])
    early, near = lax.optimization_barrier((early, partner(table)))
    mid_pack = packed(mid_tiles, mid_smoother, others[0])
    low_pack = packed(coarse_tiles, coarse_smoother, others[0])
    early, mid_pack, low_pack = lax.optimization_barrier((early, mid_pack, low_pack))
    cut = others[1].shape[0] // n1
    sums = pair_sums(own, early, pairs - 1, n1) + pair_sums(own, late, cut - 1, n1)
    sums = sums[::-1]
    tables = [near, forwarded(near)]
    terms = [sums[0]] + [lax.ppermute(sums[k], "blk", steps[k]) for k in range(1, pairs)]
    terms, tables = lax.optimization_barrier((terms, tables))

    mid_rhs, w, h = add_and_smooth(mid_pack, terms)
    before, after = halos(h)
    w, h = small_sweep(True, cols1, (before, h, after), mid_pack, mid_rhs, w)[::-1]
    before, after = halos(h)
    cuts = mid_restrict(cols1, mid_map, (before, h, after), mid_pack, mid_rhs, mid_slots, n2)

    shifts = [[(i, (i + k) % folds) for i in range(folds)] for k in range(folds)]
    terms = [cuts[0]] + [lax.ppermute(cuts[k], "fold", shifts[k]) for k in range(1, folds)]
    low_rhs, c, h = add_and_smooth(low_pack, terms)
    for k in range(1, COARSE):
        before, after = halos(h)
        h, *c = small_sweep(
            False, cols2, (before, h, after), low_pack, low_rhs, c, last=k == COARSE - 1
        )
        c = c[0] if c else None
    parts = [h] + [lax.ppermute(h, "fold", shifts[k]) for k in range(1, folds)]

    coarse_field, w, h = mid_lift(mid_map, parts, w, mid_slots)
    before, after = halos(h)
    h, mid_field = small_sweep(True, cols1, (before, h, after), mid_pack, mid_rhs, w)

    far_mids = [lax.ppermute(h, "blk", steps[k]) for k in range(pairs - 1, 0, -1)]
    mids = [h] + far_mids[::-1]
    mids = mids + [partner(m) for m in far_mids + [h]][::-1]
    fine_field, mid_field, coarse_field = fine_last(
        cols0,
        fine_map,
        fine_slots,
        tables,
        mids,
        fine_pack,
        resid,
        down,
        (mid_field, coarse_field),
    )
    return fine_field, mid_field, coarse_field


def solution(mesh):
    both = ("fold", "blk")
    return jax.shard_map(
        on_device,
        mesh=mesh,
        in_specs=(
            P(both, None, None),
            P(both, None, None, None),
            P(both, None),
            P(both, None, None),
            P(both),
            P(both, None),
            P(both, None, None, None),
            P(both, None),
            P(both, None, None),
            P(both),
            P(both, None),
            P("blk", None, None, None),
            P("blk", None),
            P("blk", None, None),
        ),
        out_specs=(P(both, None, None), P(both, None, None), P("blk", None, None)),
        check_vma=False,
    )
```

profile of v0, /device:TPU:0, one launch (start us, length us, event | category | flops | bytes accessed | tf_op | source)
XLA Modules:
  0.0 180.2 jit_solution(3512592539795514798)
XLA Ops:
  3.8 3.0 %collective-permute-start = (bf16[12,32,128]{2,1,0:T(8,128)(2,1)S(1)}, bf16[12,32,128]{2,1,0:T(8,128)(2,1)S(1)}, u32[]{:S(2)}, u32[]{:S(2)}) collective-permute-start(bf16[12,32,128]{2,1,0:T(8,128)(2,1)S(1)} %get-tuple-element.64.refs_0_), channel_id=1, source_target_pairs={{0,1},{1,0},{2,3},{3,2},{4,5},{5,4},{6,7},{7,6},{8,9},{9,8},{10,11... | collective-permute-start | bytes 294920 | tf_op jit(solution)/shard_map/ppermute | solution.py:98
  7.6 2.0 %collective-permute-start.3 = (bf16[12,32,128]{2,1,0:T(8,128)(2,1)S(1)}, bf16[12,32,128]{2,1,0:T(8,128)(2,1)S(1)}, u32[]{:S(2)}, u32[]{:S(2)}) collective-permute-start(bf16[12,32,128]{2,1,0:T(8,128)(2,1)S(1)} %get-tuple-element.67.refs_3_), channel_id=1, source_target_pairs={{0,1},{1,0},{2,3},{3,2},{4,5},{5,4},{6,7},{7,6},{8,9},{9,8},{10,11... | collective-permute-start | bytes 294920 | tf_op jit(solution)/shard_map/ppermute | solution.py:98
  18.4 3.2 %copy-done.4 = bf16[48,5,128,128]{3,2,1,0:T(8,128)(2,1)S(1)} copy-done((bf16[48,5,128,128]{3,2,1,0:T(8,128)(2,1)S(1)}, bf16[48,5,128,128]{3,2,1,0:T(8,128)(2,1)}, u32[]{:S(2)}) %copy-start.4) | copy-done | bytes 7864344
  21.6 2.6 %shard_map.159.refs_12_.t_ref = bf16[48,5,128,128]{3,2,1,0:T(8,128)(2,1)S(1)} custom-call(bf16[48,5,128,128]{3,2,1,0:T(8,128)(2,1)S(1)} %copy-done.4, bf16[12,32,128]{2,1,0:T(8,128)(2,1)S(1)} %collective-permute-done.4.after_ref.refs_8_), custom_call_target="tpu_custom_call" | custom-call | bytes 9000000 | tf_op jit(solution)/shard_map/pallas_call | solution.py:165
  24.3 2.7 %shard_map.161 = (f32[24,32,128]{2,1,0:T(8,128)S(1)}, bf16[12,32,128]{2,1,0:T(8,128)(2,1)S(1)}, bf16[12,32,128]{2,1,0:T(8,128)(2,1)S(1)}) custom-call(s32[5,48]{1,0:T(8,128)S(1)} %bitcast.11, bf16[12,32,128]{2,1,0:T(8,128)(2,1)S(1)} %get-tuple-element.64.refs_0_, bf16[12,32,128]{2,1,0:T(8,128)(2,1)S(1)} %get-tuple-element.65.refs_1_, ...), custom_call_target="tpu_custom_call" | custom-call | bytes 10799999 | tf_op jit(solution)/shard_map/pallas_call | solution.py:207
  27.0 3.0 %collective-permute-start.10 = (bf16[12,32,128]{2,1,0:T(8,128)(2,1)S(1)}, bf16[12,32,128]{2,1,0:T(8,128)(2,1)S(1)}, u32[]{:S(2)}, u32[]{:S(2)}) collective-permute-start(bf16[12,32,128]{2,1,0:T(8,128)(2,1)S(1)} %get-tuple-element.72.refs_2_), channel_id=1, source_target_pairs={{0,1},{1,0},{2,3},{3,2},{4,5},{5,4},{6,7},{7,6},{8,9},{9,8},{10,11... | collective-permute-start | bytes 294920 | tf_op jit(solution)/shard_map/ppermute | solution.py:98
  30.1 2.7 %shard_map.160 = (f32[24,32,128]{2,1,0:T(8,128)S(1)}, bf16[12,32,128]{2,1,0:T(8,128)(2,1)S(1)}, bf16[12,32,128]{2,1,0:T(8,128)(2,1)S(1)}) custom-call(s32[5,48]{1,0:T(8,128)S(1)} %bitcast.12, bf16[12,32,128]{2,1,0:T(8,128)(2,1)S(1)} %get-tuple-element.64.refs_0_, bf16[12,32,128]{2,1,0:T(8,128)(2,1)S(1)} %get-tuple-element.65.refs_1_, ...), custom_call_target="tpu_custom_call" | custom-call | bytes 10799999 | tf_op jit(solution)/shard_map/pallas_call | solution.py:207
  32.8 2.0 %collective-permute-start.8 = (bf16[12,32,128]{2,1,0:T(8,128)(2,1)S(1)}, bf16[12,32,128]{2,1,0:T(8,128)(2,1)S(1)}, u32[]{:S(2)}, u32[]{:S(2)}) collective-permute-start(bf16[12,32,128]{2,1,0:T(8,128)(2,1)S(1)} %get-tuple-element.69.refs_0_), channel_id=1, source_target_pairs={{0,1},{1,0},{2,3},{3,2},{4,5},{5,4},{6,7},{7,6},{8,9},{9,8},{10,11... | collective-permute-start | bytes 294920 | tf_op jit(solution)/shard_map/ppermute | solution.py:98
  40.4 5.0 %shard_map.162.refs_12_.refs_8_ = bf16[48,6,128,128]{3,2,1,0:T(8,128)(2,1)S(1)} custom-call(bf16[48,5,128,128]{3,2,1,0:T(8,128)(2,1)S(1)} %shard_map.159.refs_12_.t_ref, bf16[48,128,128]{2,1,0:T(8,128)(2,1)S(1)} %copy-done.1, bf16[12,32,128]{2,1,0:T(8,128)(2,1)S(1)} %collective-permute-done.11.after_ref.refs_7_), custom_call_target="tpu_custom_call" | custom-call | bytes 6000000 | tf_op jit(solution)/shard_map/pallas_call | solution.py:441
  46.2 3.9 %shard_map.163 = (f32[48,32,128]{2,1,0:T(8,128)S(1)}, f32[48,32,128]{2,1,0:T(8,128)S(1)}, bf16[24,32,128]{2,1,0:T(8,128)(2,1)S(1)}, bf16[24,32,128]{2,1,0:T(8,128)(2,1)S(1)}, s32[49,128]{1,0:T(8,128)S(1)}) custom-call(s32[5,48]{1,0:T(8,128)S(1)} %bitcast.13, s32[48]{0:T(128)S(1)} %copy-done.14, bf16[12,32,128]{2,1,0:T(8,128)(2,1)S(1)} %get-tuple-element.69.refs_0_, ...), custom_call_target="tpu_custom_call" | custom-call | bytes 21600000 | tf_op jit(solution)/shard_map/pallas_call | solution.py:279
  57.3 2.3 %collective-permute-done.19.near_to_ref.near_ref = s32[49,128]{1,0:T(8,128)S(1)} collective-permute-done((s32[49,128]{1,0:T(8,128)S(1)}, s32[49,128]{1,0:T(8,128)S(1)}, u32[]{:S(2)}, u32[]{:S(2)}) %collective-permute-start.19) | collective-permute-done | bytes 25120 | tf_op jit(solution)/shard_map/ppermute | solution.py:98
  62.3 5.1 %collective-permute-done.22.far_to_ref.far_ref = s32[49,128]{1,0:T(8,128)S(1)} collective-permute-done((s32[49,128]{1,0:T(8,128)S(1)}, s32[49,128]{1,0:T(8,128)S(1)}, u32[]{:S(2)}, u32[]{:S(2)}) %collective-permute-start.22) | collective-permute-done | bytes 25120 | tf_op jit(solution)/shard_map/ppermute | solution.py:103
  67.7 4.7 %collective-permute-start.23 = (bf16[12,32,128]{2,1,0:T(8,128)(2,1)S(1)}, bf16[12,32,128]{2,1,0:T(8,128)(2,1)S(1)}, u32[]{:S(2)}, u32[]{:S(2)}) collective-permute-start(bf16[12,32,128]{2,1,0:T(8,128)(2,1)S(1)} %get-tuple-element.93.b_ref), channel_id=1, source_target_pairs={{1,0},{2,1},{3,2},{4,3},{5,4},{6,5},{7,6},{0,7},{9,8},{10,9},{11,1... | collective-permute-start | bytes 294920 | tf_op jit(solution)/shard_map/ppermute | solution.py:93
  72.4 2.6 %collective-permute-done.24.a_ref = bf16[12,32,128]{2,1,0:T(8,128)(2,1)S(1)} collective-permute-done((bf16[12,32,128]{2,1,0:T(8,128)(2,1)S(1)}, bf16[12,32,128]{2,1,0:T(8,128)(2,1)S(1)}, u32[]{:S(2)}, u32[]{:S(2)}) %collective-permute-start.24) | collective-permute-done | bytes 98336 | tf_op jit(solution)/shard_map/ppermute | solution.py:93
  76.2 4.8 %collective-permute-start.25 = (bf16[12,32,128]{2,1,0:T(8,128)(2,1)S(1)}, bf16[12,32,128]{2,1,0:T(8,128)(2,1)S(1)}, u32[]{:S(2)}, u32[]{:S(2)}) collective-permute-start(bf16[12,32,128]{2,1,0:T(8,128)(2,1)S(1)} %get-tuple-element.96.b_ref), channel_id=1, source_target_pairs={{1,0},{2,1},{3,2},{4,3},{5,4},{6,5},{7,6},{0,7},{9,8},{10,9},{11,1... | collective-permute-start | bytes 294920 | tf_op jit(solution)/shard_map/ppermute | solution.py:93
  81.0 2.5 %collective-permute-done.26.a_ref = bf16[12,32,128]{2,1,0:T(8,128)(2,1)S(1)} collective-permute-done((bf16[12,32,128]{2,1,0:T(8,128)(2,1)S(1)}, bf16[12,32,128]{2,1,0:T(8,128)(2,1)S(1)}, u32[]{:S(2)}, u32[]{:S(2)}) %collective-permute-start.26) | collective-permute-done | bytes 98336 | tf_op jit(solution)/shard_map/ppermute | solution.py:93
  90.0 4.5 %collective-permute-start.30 = (bf16[12,8,128]{2,1,0:T(8,128)(2,1)S(1)}, bf16[12,8,128]{2,1,0:T(8,128)(2,1)S(1)}, u32[]{:S(2)}, u32[]{:S(2)}) collective-permute-start(bf16[12,8,128]{2,1,0:T(8,128)(2,1)S(1)} %get-tuple-element.101.b_ref), channel_id=1, source_target_pairs={{1,0},{2,1},{3,2},{4,3},{5,4},{6,5},{7,6},{0,7},{9,8},{10,9},{11,1... | collective-permute-start | bytes 73736 | tf_op jit(solution)/shard_map/ppermute | solution.py:93
  94.5 1.9 %collective-permute-done.31.a_ref = bf16[12,8,128]{2,1,0:T(8,128)(2,1)S(1)} collective-permute-done((bf16[12,8,128]{2,1,0:T(8,128)(2,1)S(1)}, bf16[12,8,128]{2,1,0:T(8,128)(2,1)S(1)}, u32[]{:S(2)}, u32[]{:S(2)}) %collective-permute-start.31) | collective-permute-done | bytes 24608 | tf_op jit(solution)/shard_map/ppermute | solution.py:93
  97.6 4.7 %collective-permute-start.32 = (bf16[12,8,128]{2,1,0:T(8,128)(2,1)S(1)}, bf16[12,8,128]{2,1,0:T(8,128)(2,1)S(1)}, u32[]{:S(2)}, u32[]{:S(2)}) collective-permute-start(bf16[12,8,128]{2,1,0:T(8,128)(2,1)S(1)} %get-tuple-element.104.b_ref), channel_id=1, source_target_pairs={{1,0},{2,1},{3,2},{4,3},{5,4},{6,5},{7,6},{0,7},{9,8},{10,9},{11,1... | collective-permute-start | bytes 73736 | tf_op jit(solution)/shard_map/ppermute | solution.py:93
  105.3 4.8 %collective-permute-start.34 = (bf16[12,8,128]{2,1,0:T(8,128)(2,1)S(1)}, bf16[12,8,128]{2,1,0:T(8,128)(2,1)S(1)}, u32[]{:S(2)}, u32[]{:S(2)}) collective-permute-start(bf16[12,8,128]{2,1,0:T(8,128)(2,1)S(1)} %get-tuple-element.106.b_ref), channel_id=1, source_target_pairs={{1,0},{2,1},{3,2},{4,3},{5,4},{6,5},{7,6},{0,7},{9,8},{10,9},{11,1... | collective-permute-start | bytes 73736 | tf_op jit(solution)/shard_map/ppermute | solution.py:93
  113.0 4.8 %collective-permute-start.36 = (bf16[12,8,128]{2,1,0:T(8,128)(2,1)S(1)}, bf16[12,8,128]{2,1,0:T(8,128)(2,1)S(1)}, u32[]{:S(2)}, u32[]{:S(2)}) collective-permute-start(bf16[12,8,128]{2,1,0:T(8,128)(2,1)S(1)} %get-tuple-element.108.b_ref), channel_id=1, source_target_pairs={{1,0},{2,1},{3,2},{4,3},{5,4},{6,5},{7,6},{0,7},{9,8},{10,9},{11,1... | collective-permute-start | bytes 73736 | tf_op jit(solution)/shard_map/ppermute | solution.py:93
  120.8 4.8 %collective-permute-start.38 = (bf16[12,8,128]{2,1,0:T(8,128)(2,1)S(1)}, bf16[12,8,128]{2,1,0:T(8,128)(2,1)S(1)}, u32[]{:S(2)}, u32[]{:S(2)}) collective-permute-start(bf16[12,8,128]{2,1,0:T(8,128)(2,1)S(1)} %get-tuple-element.110.b_ref), channel_id=1, source_target_pairs={{1,0},{2,1},{3,2},{4,3},{5,4},{6,5},{7,6},{0,7},{9,8},{10,9},{11,1... | collective-permute-start | bytes 73736 | tf_op jit(solution)/shard_map/ppermute | solution.py:93
  128.5 4.8 %collective-permute-start.40 = (bf16[12,8,128]{2,1,0:T(8,128)(2,1)S(1)}, bf16[12,8,128]{2,1,0:T(8,128)(2,1)S(1)}, u32[]{:S(2)}, u32[]{:S(2)}) collective-permute-start(bf16[12,8,128]{2,1,0:T(8,128)(2,1)S(1)} %get-tuple-element.112.b_ref), channel_id=1, source_target_pairs={{1,0},{2,1},{3,2},{4,3},{5,4},{6,5},{7,6},{0,7},{9,8},{10,9},{11,1... | collective-permute-start | bytes 73736 | tf_op jit(solution)/shard_map/ppermute | solution.py:93
  136.5 4.8 %collective-permute-start.42 = (bf16[12,8,128]{2,1,0:T(8,128)(2,1)S(1)}, bf16[12,8,128]{2,1,0:T(8,128)(2,1)S(1)}, u32[]{:S(2)}, u32[]{:S(2)}) collective-permute-start(bf16[12,8,128]{2,1,0:T(8,128)(2,1)S(1)} %get-tuple-element.114.b_ref), channel_id=1, source_target_pairs={{1,0},{2,1},{3,2},{4,3},{5,4},{6,5},{7,6},{0,7},{9,8},{10,9},{11,1... | collective-permute-start | bytes 73736 | tf_op jit(solution)/shard_map/ppermute | solution.py:93
  145.8 2.4 %collective-permute-done.45.refs_2_ = bf16[12,8,128]{2,1,0:T(8,128)(2,1)S(1)} collective-permute-done((bf16[12,8,128]{2,1,0:T(8,128)(2,1)S(1)}, bf16[12,8,128]{2,1,0:T(8,128)(2,1)S(1)}, u32[]{:S(2)}, u32[]{:S(2)}) %collective-permute-start.45) | collective-permute-done | bytes 24608 | tf_op jit(solution)/shard_map/ppermute | solution.py:640
  149.2 4.8 %collective-permute-start.47 = (bf16[12,32,128]{2,1,0:T(8,128)(2,1)S(1)}, bf16[12,32,128]{2,1,0:T(8,128)(2,1)S(1)}, u32[]{:S(2)}, u32[]{:S(2)}) collective-permute-start(bf16[12,32,128]{2,1,0:T(8,128)(2,1)S(1)} %get-tuple-element.117.b_ref), channel_id=1, source_target_pairs={{1,0},{2,1},{3,2},{4,3},{5,4},{6,5},{7,6},{0,7},{9,8},{10,9},{11,1... | collective-permute-start | bytes 294920 | tf_op jit(solution)/shard_map/ppermute | solution.py:93
  154.1 2.5 %collective-permute-done.48.a_ref = bf16[12,32,128]{2,1,0:T(8,128)(2,1)S(1)} collective-permute-done((bf16[12,32,128]{2,1,0:T(8,128)(2,1)S(1)}, bf16[12,32,128]{2,1,0:T(8,128)(2,1)S(1)}, u32[]{:S(2)}, u32[]{:S(2)}) %collective-permute-start.48) | collective-permute-done | bytes 98336 | tf_op jit(solution)/shard_map/ppermute | solution.py:93
  157.9 3.1 %collective-permute-start.51 = (bf16[12,32,128]{2,1,0:T(8,128)(2,1)S(1)}, bf16[12,32,128]{2,1,0:T(8,128)(2,1)S(1)}, u32[]{:S(2)}, u32[]{:S(2)}) collective-permute-start(bf16[12,32,128]{2,1,0:T(8,128)(2,1)S(1)} %get-tuple-element.119.refs_7_), channel_id=1, source_target_pairs={{0,4},{1,5},{2,6},{3,7},{4,0},{5,1},{6,2},{7,3},{8,12},{9,13},{10,... | collective-permute-start | bytes 294920 | tf_op jit(solution)/shard_map/ppermute | solution.py:646
  161.7 2.1 %collective-permute-start.55 = (bf16[12,32,128]{2,1,0:T(8,128)(2,1)S(1)}, bf16[12,32,128]{2,1,0:T(8,128)(2,1)S(1)}, u32[]{:S(2)}, u32[]{:S(2)}) collective-permute-start(bf16[12,32,128]{2,1,0:T(8,128)(2,1)S(1)} %get-tuple-element.119.refs_7_), channel_id=1, source_target_pairs={{0,1},{1,0},{2,3},{3,2},{4,5},{5,4},{6,7},{7,6},{8,9},{9,8},{10,11... | collective-permute-start | bytes 294920 | tf_op jit(solution)/shard_map/ppermute | solution.py:98
  166.9 2.6 %collective-permute-start.52 = (bf16[12,32,128]{2,1,0:T(8,128)(2,1)S(1)}, bf16[12,32,128]{2,1,0:T(8,128)(2,1)S(1)}, u32[]{:S(2)}, u32[]{:S(2)}) collective-permute-start(bf16[12,32,128]{2,1,0:T(8,128)(2,1)S(1)} %collective-permute-done.51.refs_5_), channel_id=1, source_target_pairs={{0,1},{1,0},{2,3},{3,2},{4,5},{5,4},{6,7},{7,6},{8,9},{9,8},{10,11... | collective-permute-start | bytes 294920 | tf_op jit(solution)/shard_map/ppermute | solution.py:98
  169.9 2.6 %collective-permute-done.52.refs_1_ = bf16[12,32,128]{2,1,0:T(8,128)(2,1)S(1)} collective-permute-done((bf16[12,32,128]{2,1,0:T(8,128)(2,1)S(1)}, bf16[12,32,128]{2,1,0:T(8,128)(2,1)S(1)}, u32[]{:S(2)}, u32[]{:S(2)}) %collective-permute-start.52) | collective-permute-done | bytes 98336 | tf_op jit(solution)/shard_map/ppermute | solution.py:98
  174.0 6.0 %shard_map.181 = (f32[48,32,128]{2,1,0:T(8,128)}, f32[12,32,128]{2,1,0:T(8,128)}, f32[12,32,128]{2,1,0:T(8,128)}) custom-call(s32[5,48]{1,0:T(8,128)S(1)} %bitcast.14, s32[48]{0:T(128)S(1)} %copy-done.14, s32[49,128]{1,0:T(8,128)S(1)} %collective-permute-done.19.near_to_ref.near_ref, s32[49,128]{1,0:T(8,128)S(1)} %collective-permute-done.22.far_to_ref.far_ref, ...), custom_call_target="tpu_custom_call" | custom-call | bytes 28800000 | tf_op jit(solution)/shard_map/pallas_call | solution.py:401
  (137 shorter events, 65.3 us)
Async XLA Ops:
  7.6 7.4 %collective-permute-start.3 = (bf16[12,32,128]{2,1,0:T(8,128)(2,1)S(1)}, bf16[12,32,128]{2,1,0:T(8,128)(2,1)S(1)}, u32[]{:S(2)}, u32[]{:S(2)}) collective-permute-start(bf16[12,32,128]{2,1,0:T(8,128)(2,1)S(1)} %get-tuple-element.67.refs_3_), channel_id=1, source_target_pairs={{0,1},{1,0},{2,3},{3,2},{4,5},{5,4},{6,7},{7,6},{8,9},{9,8},{10,11... | collective-permute-start | bytes 294920 | tf_op jit(solution)/shard_map/ppermute | solution.py:98
  9.6 7.2 %collective-permute-start.1 = (bf16[12,32,128]{2,1,0:T(8,128)(2,1)S(1)}, bf16[12,32,128]{2,1,0:T(8,128)(2,1)S(1)}, u32[]{:S(2)}, u32[]{:S(2)}) collective-permute-start(bf16[12,32,128]{2,1,0:T(8,128)(2,1)S(1)} %get-tuple-element.65.refs_1_), channel_id=1, source_target_pairs={{0,1},{1,0},{2,3},{3,2},{4,5},{5,4},{6,7},{7,6},{8,9},{9,8},{10,11... | collective-permute-start | bytes 294920 | tf_op jit(solution)/shard_map/ppermute | solution.py:98
  10.1 8.3 %collective-permute-start.4 = (bf16[12,32,128]{2,1,0:T(8,128)(2,1)S(1)}, bf16[12,32,128]{2,1,0:T(8,128)(2,1)S(1)}, u32[]{:S(2)}, u32[]{:S(2)}) collective-permute-start(bf16[12,32,128]{2,1,0:T(8,128)(2,1)S(1)} %collective-permute-done.refs_4_), channel_id=1, source_target_pairs={{0,2},{1,7},{2,4},{3,1},{4,6},{5,3},{6,0},{7,5},{8,10},{9,15},{10,... | collective-permute-start | bytes 294920 | tf_op jit(solution)/shard_map/ppermute | solution.py:103
  13.3 10.9 %collective-permute-start.6 = (bf16[12,32,128]{2,1,0:T(8,128)(2,1)S(1)}, bf16[12,32,128]{2,1,0:T(8,128)(2,1)S(1)}, u32[]{:S(2)}, u32[]{:S(2)}) collective-permute-start(bf16[12,32,128]{2,1,0:T(8,128)(2,1)S(1)} %collective-permute-done.2.refs_6_), channel_id=1, source_target_pairs={{0,2},{1,7},{2,4},{3,1},{4,6},{5,3},{6,0},{7,5},{8,10},{9,15},{10,... | collective-permute-start | bytes 294920 | tf_op jit(solution)/shard_map/ppermute | solution.py:103
  15.0 9.2 %collective-permute-start.7 = (bf16[12,32,128]{2,1,0:T(8,128)(2,1)S(1)}, bf16[12,32,128]{2,1,0:T(8,128)(2,1)S(1)}, u32[]{:S(2)}, u32[]{:S(2)}) collective-permute-start(bf16[12,32,128]{2,1,0:T(8,128)(2,1)S(1)} %collective-permute-done.3.refs_7_), channel_id=1, source_target_pairs={{0,2},{1,7},{2,4},{3,1},{4,6},{5,3},{6,0},{7,5},{8,10},{9,15},{10,... | collective-permute-start | bytes 294920 | tf_op jit(solution)/shard_map/ppermute | solution.py:103
  16.8 7.4 %collective-permute-start.5 = (bf16[12,32,128]{2,1,0:T(8,128)(2,1)S(1)}, bf16[12,32,128]{2,1,0:T(8,128)(2,1)S(1)}, u32[]{:S(2)}, u32[]{:S(2)}) collective-permute-start(bf16[12,32,128]{2,1,0:T(8,128)(2,1)S(1)} %collective-permute-done.1.refs_5_), channel_id=1, source_target_pairs={{0,2},{1,7},{2,4},{3,1},{4,6},{5,3},{6,0},{7,5},{8,10},{9,15},{10,... | collective-permute-start | bytes 294920 | tf_op jit(solution)/shard_map/ppermute | solution.py:103
  27.0 7.9 %collective-permute-start.10 = (bf16[12,32,128]{2,1,0:T(8,128)(2,1)S(1)}, bf16[12,32,128]{2,1,0:T(8,128)(2,1)S(1)}, u32[]{:S(2)}, u32[]{:S(2)}) collective-permute-start(bf16[12,32,128]{2,1,0:T(8,128)(2,1)S(1)} %get-tuple-element.72.refs_2_), channel_id=1, source_target_pairs={{0,1},{1,0},{2,3},{3,2},{4,5},{5,4},{6,7},{7,6},{8,9},{9,8},{10,11... | collective-permute-start | bytes 294920 | tf_op jit(solution)/shard_map/ppermute | solution.py:98
  34.9 10.6 %collective-permute-start.14 = (bf16[12,32,128]{2,1,0:T(8,128)(2,1)S(1)}, bf16[12,32,128]{2,1,0:T(8,128)(2,1)S(1)}, u32[]{:S(2)}, u32[]{:S(2)}) collective-permute-start(bf16[12,32,128]{2,1,0:T(8,128)(2,1)S(1)} %collective-permute-done.10.refs_6_), channel_id=1, source_target_pairs={{0,2},{1,7},{2,4},{3,1},{4,6},{5,3},{6,0},{7,5},{8,10},{9,15},{10,... | collective-permute-start | bytes 294920 | tf_op jit(solution)/shard_map/ppermute | solution.py:103
  35.9 9.6 %collective-permute-start.15 = (bf16[12,32,128]{2,1,0:T(8,128)(2,1)S(1)}, bf16[12,32,128]{2,1,0:T(8,128)(2,1)S(1)}, u32[]{:S(2)}, u32[]{:S(2)}) collective-permute-start(bf16[12,32,128]{2,1,0:T(8,128)(2,1)S(1)} %collective-permute-done.11.after_ref.refs_7_), channel_id=1, source_target_pairs={{0,2},{1,7},{2,4},{3,1},{4,6},{5,3},{6,0},{7,5},{8,10},{9,15},{10,... | collective-permute-start | bytes 294920 | tf_op jit(solution)/shard_map/ppermute | solution.py:103
  37.8 7.7 %collective-permute-start.12 = (bf16[12,32,128]{2,1,0:T(8,128)(2,1)S(1)}, bf16[12,32,128]{2,1,0:T(8,128)(2,1)S(1)}, u32[]{:S(2)}, u32[]{:S(2)}) collective-permute-start(bf16[12,32,128]{2,1,0:T(8,128)(2,1)S(1)} %collective-permute-done.8.refs_4_), channel_id=1, source_target_pairs={{0,2},{1,7},{2,4},{3,1},{4,6},{5,3},{6,0},{7,5},{8,10},{9,15},{10,... | collective-permute-start | bytes 294920 | tf_op jit(solution)/shard_map/ppermute | solution.py:103
  39.4 6.8 %collective-permute-start.13 = (bf16[12,32,128]{2,1,0:T(8,128)(2,1)S(1)}, bf16[12,32,128]{2,1,0:T(8,128)(2,1)S(1)}, u32[]{:S(2)}, u32[]{:S(2)}) collective-permute-start(bf16[12,32,128]{2,1,0:T(8,128)(2,1)S(1)} %collective-permute-done.9.refs_5_), channel_id=1, source_target_pairs={{0,2},{1,7},{2,4},{3,1},{4,6},{5,3},{6,0},{7,5},{8,10},{9,15},{10,... | collective-permute-start | bytes 294920 | tf_op jit(solution)/shard_map/ppermute | solution.py:103
  50.2 7.0 %collective-permute-start.16 = (bf16[24,32,128]{2,1,0:T(8,128)(2,1)S(1)}, bf16[24,32,128]{2,1,0:T(8,128)(2,1)S(1)}, u32[]{:S(2)}, u32[]{:S(2)}) collective-permute-start(bf16[24,32,128]{2,1,0:T(8,128)(2,1)S(1)} %get-tuple-element.75), channel_id=1, source_target_pairs={{0,1},{1,0},{2,3},{3,2},{4,5},{5,4},{6,7},{7,6},{8,9},{9,8},{10,11... | collective-permute-start | bytes 589832 | tf_op jit(solution)/shard_map/ppermute | solution.py:98
  51.0 8.6 %collective-permute-start.18 = (bf16[24,32,128]{2,1,0:T(8,128)(2,1)S(1)}, bf16[24,32,128]{2,1,0:T(8,128)(2,1)S(1)}, u32[]{:S(2)}, u32[]{:S(2)}) collective-permute-start(bf16[24,32,128]{2,1,0:T(8,128)(2,1)S(1)} %get-tuple-element.78.after_ref), channel_id=1, source_target_pairs={{0,1},{1,0},{2,3},{3,2},{4,5},{5,4},{6,7},{7,6},{8,9},{9,8},{10,11... | collective-permute-start | bytes 589832 | tf_op jit(solution)/shard_map/ppermute | solution.py:98
  52.3 7.3 %collective-permute-start.19 = (s32[49,128]{1,0:T(8,128)S(1)}, s32[49,128]{1,0:T(8,128)S(1)}, u32[]{:S(2)}, u32[]{:S(2)}) collective-permute-start(s32[49,128]{1,0:T(8,128)S(1)} %get-tuple-element.79), channel_id=1, source_target_pairs={{0,1},{1,0},{2,3},{3,2},{4,5},{5,4},{6,7},{7,6},{8,9},{9,8},{10,11... | collective-permute-start | bytes 75272 | tf_op jit(solution)/shard_map/ppermute | solution.py:98
  57.2 10.2 %collective-permute-start.17 = (bf16[12,32,128]{2,1,0:T(8,128)(2,1)S(1)}, bf16[12,32,128]{2,1,0:T(8,128)(2,1)S(1)}, u32[]{:S(2)}, u32[]{:S(2)}) collective-permute-start(bf16[12,32,128]{2,1,0:T(8,128)(2,1)S(1)} %get-tuple-element.77), channel_id=1, source_target_pairs={{0,2},{1,3},{2,4},{3,5},{4,6},{5,7},{6,0},{7,1},{8,10},{9,11},{10,... | collective-permute-start | bytes 294920 | tf_op jit(solution)/shard_map/ppermute | solution.py:622
  59.6 7.7 %collective-permute-start.20 = (bf16[12,32,128]{2,1,0:T(8,128)(2,1)S(1)}, bf16[12,32,128]{2,1,0:T(8,128)(2,1)S(1)}, u32[]{:S(2)}, u32[]{:S(2)}) collective-permute-start(bf16[12,32,128]{2,1,0:T(8,128)(2,1)S(1)} %get-tuple-element.82), channel_id=1, source_target_pairs={{0,4},{1,5},{2,6},{3,7},{4,0},{5,1},{6,2},{7,3},{8,12},{9,13},{10,... | collective-permute-start | bytes 294920 | tf_op jit(solution)/shard_map/ppermute | solution.py:622
  60.2 7.1 %collective-permute-start.21 = (bf16[12,32,128]{2,1,0:T(8,128)(2,1)S(1)}, bf16[12,32,128]{2,1,0:T(8,128)(2,1)S(1)}, u32[]{:S(2)}, u32[]{:S(2)}) collective-permute-start(bf16[12,32,128]{2,1,0:T(8,128)(2,1)S(1)} %get-tuple-element.83), channel_id=1, source_target_pairs={{0,6},{1,7},{2,0},{3,1},{4,2},{5,3},{6,4},{7,5},{8,14},{9,15},{10,... | collective-permute-start | bytes 294920 | tf_op jit(solution)/shard_map/ppermute | solution.py:622
  67.6 7.3 %collective-permute-start.24 = (bf16[12,32,128]{2,1,0:T(8,128)(2,1)S(1)}, bf16[12,32,128]{2,1,0:T(8,128)(2,1)S(1)}, u32[]{:S(2)}, u32[]{:S(2)}) collective-permute-start(bf16[12,32,128]{2,1,0:T(8,128)(2,1)S(1)} %get-tuple-element.93.b_ref), channel_id=1, source_target_pairs={{0,1},{1,2},{2,3},{3,4},{4,5},{5,6},{6,7},{7,0},{8,9},{9,10},{10,1... | collective-permute-start | bytes 294920 | tf_op jit(solution)/shard_map/ppermute | solution.py:93
  67.7 7.3 %collective-permute-start.23 = (bf16[12,32,128]{2,1,0:T(8,128)(2,1)S(1)}, bf16[12,32,128]{2,1,0:T(8,128)(2,1)S(1)}, u32[]{:S(2)}, u32[]{:S(2)}) collective-permute-start(bf16[12,32,128]{2,1,0:T(8,128)(2,1)S(1)} %get-tuple-element.93.b_ref), channel_id=1, source_target_pairs={{1,0},{2,1},{3,2},{4,3},{5,4},{6,5},{7,6},{0,7},{9,8},{10,9},{11,1... | collective-permute-start | bytes 294920 | tf_op jit(solution)/shard_map/ppermute | solution.py:93
  76.2 7.4 %collective-permute-start.26 = (bf16[12,32,128]{2,1,0:T(8,128)(2,1)S(1)}, bf16[12,32,128]{2,1,0:T(8,128)(2,1)S(1)}, u32[]{:S(2)}, u32[]{:S(2)}) collective-permute-start(bf16[12,32,128]{2,1,0:T(8,128)(2,1)S(1)} %get-tuple-element.96.b_ref), channel_id=1, source_target_pairs={{0,1},{1,2},{2,3},{3,4},{4,5},{5,6},{6,7},{7,0},{8,9},{9,10},{10,1... | collective-permute-start | bytes 294920 | tf_op jit(solution)/shard_map/ppermute | solution.py:93
  76.2 7.3 %collective-permute-start.25 = (bf16[12,32,128]{2,1,0:T(8,128)(2,1)S(1)}, bf16[12,32,128]{2,1,0:T(8,128)(2,1)S(1)}, u32[]{:S(2)}, u32[]{:S(2)}) collective-permute-start(bf16[12,32,128]{2,1,0:T(8,128)(2,1)S(1)} %get-tuple-element.96.b_ref), channel_id=1, source_target_pairs={{1,0},{2,1},{3,2},{4,3},{5,4},{6,5},{7,6},{0,7},{9,8},{10,9},{11,1... | collective-permute-start | bytes 294920 | tf_op jit(solution)/shard_map/ppermute | solution.py:93
  89.6 6.8 %collective-permute-start.31 = (bf16[12,8,128]{2,1,0:T(8,128)(2,1)S(1)}, bf16[12,8,128]{2,1,0:T(8,128)(2,1)S(1)}, u32[]{:S(2)}, u32[]{:S(2)}) collective-permute-start(bf16[12,8,128]{2,1,0:T(8,128)(2,1)S(1)} %get-tuple-element.101.b_ref), channel_id=1, source_target_pairs={{0,1},{1,2},{2,3},{3,4},{4,5},{5,6},{6,7},{7,0},{8,9},{9,10},{10,1... | collective-permute-start | bytes 73736 | tf_op jit(solution)/shard_map/ppermute | solution.py:93
  113.0 6.6 %collective-permute-start.37 = (bf16[12,8,128]{2,1,0:T(8,128)(2,1)S(1)}, bf16[12,8,128]{2,1,0:T(8,128)(2,1)S(1)}, u32[]{:S(2)}, u32[]{:S(2)}) collective-permute-start(bf16[12,8,128]{2,1,0:T(8,128)(2,1)S(1)} %get-tuple-element.108.b_ref), channel_id=1, source_target_pairs={{0,1},{1,2},{2,3},{3,4},{4,5},{5,6},{6,7},{7,0},{8,9},{9,10},{10,1... | collective-permute-start | bytes 73736 | tf_op jit(solution)/shard_map/ppermute | solution.py:93
  120.7 6.6 %collective-permute-start.39 = (bf16[12,8,128]{2,1,0:T(8,128)(2,1)S(1)}, bf16[12,8,128]{2,1,0:T(8,128)(2,1)S(1)}, u32[]{:S(2)}, u32[]{:S(2)}) collective-permute-start(bf16[12,8,128]{2,1,0:T(8,128)(2,1)S(1)} %get-tuple-element.110.b_ref), channel_id=1, source_target_pairs={{0,1},{1,2},{2,3},{3,4},{4,5},{5,6},{6,7},{7,0},{8,9},{9,10},{10,1... | collective-permute-start | bytes 73736 | tf_op jit(solution)/shard_map/ppermute | solution.py:93
  128.5 6.6 %collective-permute-start.41 = (bf16[12,8,128]{2,1,0:T(8,128)(2,1)S(1)}, bf16[12,8,128]{2,1,0:T(8,128)(2,1)S(1)}, u32[]{:S(2)}, u32[]{:S(2)}) collective-permute-start(bf16[12,8,128]{2,1,0:T(8,128)(2,1)S(1)} %get-tuple-element.112.b_ref), channel_id=1, source_target_pairs={{0,1},{1,2},{2,3},{3,4},{4,5},{5,6},{6,7},{7,0},{8,9},{9,10},{10,1... | collective-permute-start | bytes 73736 | tf_op jit(solution)/shard_map/ppermute | solution.py:93
  136.3 6.8 %collective-permute-start.43 = (bf16[12,8,128]{2,1,0:T(8,128)(2,1)S(1)}, bf16[12,8,128]{2,1,0:T(8,128)(2,1)S(1)}, u32[]{:S(2)}, u32[]{:S(2)}) collective-permute-start(bf16[12,8,128]{2,1,0:T(8,128)(2,1)S(1)} %get-tuple-element.114.b_ref), channel_id=1, source_target_pairs={{0,1},{1,2},{2,3},{3,4},{4,5},{5,6},{6,7},{7,0},{8,9},{9,10},{10,1... | collective-permute-start | bytes 73736 | tf_op jit(solution)/shard_map/ppermute | solution.py:93
  149.2 7.4 %collective-permute-start.48 = (bf16[12,32,128]{2,1,0:T(8,128)(2,1)S(1)}, bf16[12,32,128]{2,1,0:T(8,128)(2,1)S(1)}, u32[]{:S(2)}, u32[]{:S(2)}) collective-permute-start(bf16[12,32,128]{2,1,0:T(8,128)(2,1)S(1)} %get-tuple-element.117.b_ref), channel_id=1, source_target_pairs={{0,1},{1,2},{2,3},{3,4},{4,5},{5,6},{6,7},{7,0},{8,9},{9,10},{10,1... | collective-permute-start | bytes 294920 | tf_op jit(solution)/shard_map/ppermute | solution.py:93
  149.2 7.4 %collective-permute-start.47 = (bf16[12,32,128]{2,1,0:T(8,128)(2,1)S(1)}, bf16[12,32,128]{2,1,0:T(8,128)(2,1)S(1)}, u32[]{:S(2)}, u32[]{:S(2)}) collective-permute-start(bf16[12,32,128]{2,1,0:T(8,128)(2,1)S(1)} %get-tuple-element.117.b_ref), channel_id=1, source_target_pairs={{1,0},{2,1},{3,2},{4,3},{5,4},{6,5},{7,6},{0,7},{9,8},{10,9},{11,1... | collective-permute-start | bytes 294920 | tf_op jit(solution)/shard_map/ppermute | solution.py:93
  157.8 6.9 %collective-permute-start.53 = (bf16[12,32,128]{2,1,0:T(8,128)(2,1)S(1)}, bf16[12,32,128]{2,1,0:T(8,128)(2,1)S(1)}, u32[]{:S(2)}, u32[]{:S(2)}) collective-permute-start(bf16[12,32,128]{2,1,0:T(8,128)(2,1)S(1)} %get-tuple-element.119.refs_7_), channel_id=1, source_target_pairs={{0,2},{1,3},{2,4},{3,5},{4,6},{5,7},{6,0},{7,1},{8,10},{9,11},{10,... | collective-permute-start | bytes 294920 | tf_op jit(solution)/shard_map/ppermute | solution.py:646
  157.9 9.0 %collective-permute-start.51 = (bf16[12,32,128]{2,1,0:T(8,128)(2,1)S(1)}, bf16[12,32,128]{2,1,0:T(8,128)(2,1)S(1)}, u32[]{:S(2)}, u32[]{:S(2)}) collective-permute-start(bf16[12,32,128]{2,1,0:T(8,128)(2,1)S(1)} %get-tuple-element.119.refs_7_), channel_id=1, source_target_pairs={{0,4},{1,5},{2,6},{3,7},{4,0},{5,1},{6,2},{7,3},{8,12},{9,13},{10,... | collective-permute-start | bytes 294920 | tf_op jit(solution)/shard_map/ppermute | solution.py:646
  161.0 8.4 %collective-permute-start.49 = (bf16[12,32,128]{2,1,0:T(8,128)(2,1)S(1)}, bf16[12,32,128]{2,1,0:T(8,128)(2,1)S(1)}, u32[]{:S(2)}, u32[]{:S(2)}) collective-permute-start(bf16[12,32,128]{2,1,0:T(8,128)(2,1)S(1)} %get-tuple-element.119.refs_7_), channel_id=1, source_target_pairs={{0,6},{1,7},{2,0},{3,1},{4,2},{5,3},{6,4},{7,5},{8,14},{9,15},{10,... | collective-permute-start | bytes 294920 | tf_op jit(solution)/shard_map/ppermute | solution.py:646
  161.7 7.8 %collective-permute-start.55 = (bf16[12,32,128]{2,1,0:T(8,128)(2,1)S(1)}, bf16[12,32,128]{2,1,0:T(8,128)(2,1)S(1)}, u32[]{:S(2)}, u32[]{:S(2)}) collective-permute-start(bf16[12,32,128]{2,1,0:T(8,128)(2,1)S(1)} %get-tuple-element.119.refs_7_), channel_id=1, source_target_pairs={{0,1},{1,0},{2,3},{3,2},{4,5},{5,4},{6,7},{7,6},{8,9},{9,8},{10,11... | collective-permute-start | bytes 294920 | tf_op jit(solution)/shard_map/ppermute | solution.py:98
  (40 other events, 289.0 us)
where the time goes:
time: 180 us
  starting transfers between devices  88.6 us (49%)
  waiting for transfers between devices  44.7 us (25%)
  Pallas kernels  39.8 us (22%)
  local copies, waits for them, and re-layouts  5.82 us (3%)
    ppermute x20, starting transfers between devices, halos(): return (lax.ppermute(value, 'blk', up), lax.ppermute(value, 'blk', down))  48.5 us
    ppermute x20, waiting for transfers between devices, halos(): return (lax.ppermute(value, 'blk', up), lax.ppermute(value, 'blk', down))  20.1 us
    ppermute x15, starting transfers between devices, partner(): return lax.ppermute(value, 'blk', [(i, i ^ 1) for i in range(n)])  19.5 us
    ppermute x15, waiting for transfers between devices, partner(): return lax.ppermute(value, 'blk', [(i, i ^ 1) for i in range(n)])  12.7 us
    ppermute x9, starting transfers between devices, forwarded(): lax.ppermute(value, 'blk', [(i, (i + 2 - 4 * (i % 2)) % n) for i in range...  10.6 us
    pallas_call x9, Pallas kernels, small_sweep(): pl.pallas_call(kernel, in_specs=[SMEM] + [VMEM] * 6, out_specs=[VMEM] * l...  10.4 us
    pallas_call x3, Pallas kernels, packed(): pl.pallas_call(kernel, in_specs=[VMEM] * 2 + [ANY], out_specs=VMEM, out_s...  7.57 us
    pallas_call x1, Pallas kernels, fine_last(): pl.pallas_call(kernel, in_specs=[SMEM] * 4 + [VMEM] * (5 + parts + len(fi...  6 us
  transfers between devices with their start and end apart: 56, of which 30 were waited for; matrix products, arithmetic and copies ran while one was open for 0% of the time, Pallas kernels for 8%

commit v1 on v0

--- a/solution.py
+++ b/solution.py
@@ -618,9 +618,7 @@
     cut = others[1].shape[0] // n1
     sums = pair_sums(own, early, pairs - 1, n1) + pair_sums(own, late, cut - 1, n1)
     sums = sums[::-1]
-    tables = [near, forwarded(near)]
     terms = [sums[0]] + [lax.ppermute(sums[k], "blk", steps[k]) for k in range(1, pairs)]
-    terms, tables = lax.optimization_barrier((terms, tables))
 
     mid_rhs, w, h = add_and_smooth(mid_pack, terms)
     before, after = halos(h)
@@ -630,6 +628,8 @@
 
     shifts = [[(i, (i + k) % folds) for i in range(folds)] for k in range(folds)]
     terms = [cuts[0]] + [lax.ppermute(cuts[k], "fold", shifts[k]) for k in range(1, folds)]
+    terms, far = lax.optimization_barrier((terms, forwarded(near)))
+    tables = [near, far]
     low_rhs, c, h = add_and_smooth(low_pack, terms)
     for k in range(1, COARSE):
         before, after = halos(h)

time: 180 us -> 180 us (level)
    ppermute x9, waiting for transfers between devices: 5.82 us -> 0.72 us  [forwarded(): lax.ppermute(value, 'blk', [(i, (i + 2 - 4 * (i % 2)) % n) for i in range...]
    ppermute x3, waiting for transfers between devices: 0.01 us -> 4.32 us  [on_device(): lax.ppermute(sums[k], 'blk', steps[k])]
  transfers between devices with their start and end apart: 56 -> 56, of which waited for: 30 -> 32; matrix products, arithmetic and copies ran while one was open for 0% -> 0% of each run, Pallas kernels for 8% -> 8%
where the time goes in v1:
time: 180 us
  starting transfers between devices  89.3 us (50%)
  waiting for transfers between devices  43.4 us (24%)
  Pallas kernels  39.8 us (22%)
  local copies, waits for them, and re-layouts  5.82 us (3%)
    ppermute x20, starting transfers between devices, halos(): return (lax.ppermute(value, 'blk', up), lax.ppermute(value, 'blk', down))  48.6 us
    ppermute x20, waiting for transfers between devices, halos(): return (lax.ppermute(value, 'blk', up), lax.ppermute(value, 'blk', down))  19.7 us
    ppermute x15, starting transfers between devices, partner(): return lax.ppermute(value, 'blk', [(i, i ^ 1) for i in range(n)])  19.5 us
    ppermute x15, waiting for transfers between devices, partner(): return lax.ppermute(value, 'blk', [(i, i ^ 1) for i in range(n)])  12.6 us
    ppermute x9, starting transfers between devices, forwarded(): lax.ppermute(value, 'blk', [(i, (i + 2 - 4 * (i % 2)) % n) for i in range...  11 us
    pallas_call x9, Pallas kernels, small_sweep(): pl.pallas_call(kernel, in_specs=[SMEM] + [VMEM] * 6, out_specs=[VMEM] * l...  10.4 us
    pallas_call x3, Pallas kernels, packed(): pl.pallas_call(kernel, in_specs=[VMEM] * 2 + [ANY], out_specs=VMEM, out_s...  7.57 us
    pallas_call x1, Pallas kernels, fine_last(): pl.pallas_call(kernel, in_specs=[SMEM] * 4 + [VMEM] * (5 + parts + len(fi...  6 us
  transfers between devices with their start and end apart: 56, of which 32 were waited for; matrix products, arithmetic and copies ran while one was open for 0% of the time, Pallas kernels for 8%

profile of v1, /device:TPU:0, one launch (start us, length us, event | category | flops | bytes accessed | tf_op | source)
XLA Modules:
  0.0 179.5 jit_solution(116764055114357391)
XLA Ops:
  3.8 3.0 %collective-permute-start = (bf16[12,32,128]{2,1,0:T(8,128)(2,1)S(1)}, bf16[12,32,128]{2,1,0:T(8,128)(2,1)S(1)}, u32[]{:S(2)}, u32[]{:S(2)}) collective-permute-start(bf16[12,32,128]{2,1,0:T(8,128)(2,1)S(1)} %get-tuple-element.63.refs_0_), channel_id=1, source_target_pairs={{0,1},{1,0},{2,3},{3,2},{4,5},{5,4},{6,7},{7,6},{8,9},{9,8},{10,11... | collective-permute-start | bytes 294920 | tf_op jit(solution)/shard_map/ppermute | solution.py:98
  7.6 2.0 %collective-permute-start.3 = (bf16[12,32,128]{2,1,0:T(8,128)(2,1)S(1)}, bf16[12,32,128]{2,1,0:T(8,128)(2,1)S(1)}, u32[]{:S(2)}, u32[]{:S(2)}) collective-permute-start(bf16[12,32,128]{2,1,0:T(8,128)(2,1)S(1)} %get-tuple-element.66.refs_3_), channel_id=1, source_target_pairs={{0,1},{1,0},{2,3},{3,2},{4,5},{5,4},{6,7},{7,6},{8,9},{9,8},{10,11... | collective-permute-start | bytes 294920 | tf_op jit(solution)/shard_map/ppermute | solution.py:98
  18.4 3.2 %copy-done.4 = bf16[48,5,128,128]{3,2,1,0:T(8,128)(2,1)S(1)} copy-done((bf16[48,5,128,128]{3,2,1,0:T(8,128)(2,1)S(1)}, bf16[48,5,128,128]{3,2,1,0:T(8,128)(2,1)}, u32[]{:S(2)}) %copy-start.4) | copy-done | bytes 7864344
  21.6 2.6 %shard_map.159.refs_12_.t_ref = bf16[48,5,128,128]{3,2,1,0:T(8,128)(2,1)S(1)} custom-call(bf16[48,5,128,128]{3,2,1,0:T(8,128)(2,1)S(1)} %copy-done.4, bf16[12,32,128]{2,1,0:T(8,128)(2,1)S(1)} %collective-permute-done.4.after_ref.refs_8_), custom_call_target="tpu_custom_call" | custom-call | bytes 9000000 | tf_op jit(solution)/shard_map/pallas_call | solution.py:165
  24.3 2.7 %shard_map.161 = (f32[24,32,128]{2,1,0:T(8,128)S(1)}, bf16[12,32,128]{2,1,0:T(8,128)(2,1)S(1)}, bf16[12,32,128]{2,1,0:T(8,128)(2,1)S(1)}) custom-call(s32[5,48]{1,0:T(8,128)S(1)} %bitcast.11, bf16[12,32,128]{2,1,0:T(8,128)(2,1)S(1)} %get-tuple-element.63.refs_0_, bf16[12,32,128]{2,1,0:T(8,128)(2,1)S(1)} %get-tuple-element.64.refs_1_, ...), custom_call_target="tpu_custom_call" | custom-call | bytes 10799999 | tf_op jit(solution)/shard_map/pallas_call | solution.py:207
  27.0 3.0 %collective-permute-start.10 = (bf16[12,32,128]{2,1,0:T(8,128)(2,1)S(1)}, bf16[12,32,128]{2,1,0:T(8,128)(2,1)S(1)}, u32[]{:S(2)}, u32[]{:S(2)}) collective-permute-start(bf16[12,32,128]{2,1,0:T(8,128)(2,1)S(1)} %get-tuple-element.71.refs_2_), channel_id=1, source_target_pairs={{0,1},{1,0},{2,3},{3,2},{4,5},{5,4},{6,7},{7,6},{8,9},{9,8},{10,11... | collective-permute-start | bytes 294920 | tf_op jit(solution)/shard_map/ppermute | solution.py:98
  30.1 2.7 %shard_map.160 = (f32[24,32,128]{2,1,0:T(8,128)S(1)}, bf16[12,32,128]{2,1,0:T(8,128)(2,1)S(1)}, bf16[12,32,128]{2,1,0:T(8,128)(2,1)S(1)}) custom-call(s32[5,48]{1,0:T(8,128)S(1)} %bitcast.12, bf16[12,32,128]{2,1,0:T(8,128)(2,1)S(1)} %get-tuple-element.63.refs_0_, bf16[12,32,128]{2,1,0:T(8,128)(2,1)S(1)} %get-tuple-element.64.refs_1_, ...), custom_call_target="tpu_custom_call" | custom-call | bytes 10799999 | tf_op jit(solution)/shard_map/pallas_call | solution.py:207
  32.8 2.0 %collective-permute-start.8 = (bf16[12,32,128]{2,1,0:T(8,128)(2,1)S(1)}, bf16[12,32,128]{2,1,0:T(8,128)(2,1)S(1)}, u32[]{:S(2)}, u32[]{:S(2)}) collective-permute-start(bf16[12,32,128]{2,1,0:T(8,128)(2,1)S(1)} %get-tuple-element.68.refs_0_), channel_id=1, source_target_pairs={{0,1},{1,0},{2,3},{3,2},{4,5},{5,4},{6,7},{7,6},{8,9},{9,8},{10,11... | collective-permute-start | bytes 294920 | tf_op jit(solution)/shard_map/ppermute | solution.py:98
  40.4 5.0 %shard_map.162.refs_12_.refs_8_ = bf16[48,6,128,128]{3,2,1,0:T(8,128)(2,1)S(1)} custom-call(bf16[48,5,128,128]{3,2,1,0:T(8,128)(2,1)S(1)} %shard_map.159.refs_12_.t_ref, bf16[48,128,128]{2,1,0:T(8,128)(2,1)S(1)} %copy-done.1, bf16[12,32,128]{2,1,0:T(8,128)(2,1)S(1)} %collective-permute-done.11.after_ref.refs_7_), custom_call_target="tpu_custom_call" | custom-call | bytes 6000000 | tf_op jit(solution)/shard_map/pallas_call | solution.py:441
  46.2 3.9 %shard_map.163 = (f32[48,32,128]{2,1,0:T(8,128)S(1)}, f32[48,32,128]{2,1,0:T(8,128)S(1)}, bf16[24,32,128]{2,1,0:T(8,128)(2,1)S(1)}, bf16[24,32,128]{2,1,0:T(8,128)(2,1)S(1)}, s32[49,128]{1,0:T(8,128)S(1)}) custom-call(s32[5,48]{1,0:T(8,128)S(1)} %bitcast.13, s32[48]{0:T(128)S(1)} %copy-done.14, bf16[12,32,128]{2,1,0:T(8,128)(2,1)S(1)} %get-tuple-element.68.refs_0_, ...), custom_call_target="tpu_custom_call" | custom-call | bytes 21600000 | tf_op jit(solution)/shard_map/pallas_call | solution.py:279
  57.3 2.3 %collective-permute-done.17.near_to_ref.near_ref = s32[49,128]{1,0:T(8,128)S(1)} collective-permute-done((s32[49,128]{1,0:T(8,128)S(1)}, s32[49,128]{1,0:T(8,128)S(1)}, u32[]{:S(2)}, u32[]{:S(2)}) %collective-permute-start.17) | collective-permute-done | bytes 25120 | tf_op jit(solution)/shard_map/ppermute | solution.py:98
  61.6 2.1 %collective-permute-done.19.refs_1_ = bf16[12,32,128]{2,1,0:T(8,128)(2,1)S(1)} collective-permute-done((bf16[12,32,128]{2,1,0:T(8,128)(2,1)S(1)}, bf16[12,32,128]{2,1,0:T(8,128)(2,1)S(1)}, u32[]{:S(2)}, u32[]{:S(2)}) %collective-permute-start.19) | collective-permute-done | bytes 98336 | tf_op jit(solution)/shard_map/ppermute | solution.py:621
  63.7 2.2 %collective-permute-done.20.refs_2_ = bf16[12,32,128]{2,1,0:T(8,128)(2,1)S(1)} collective-permute-done((bf16[12,32,128]{2,1,0:T(8,128)(2,1)S(1)}, bf16[12,32,128]{2,1,0:T(8,128)(2,1)S(1)}, u32[]{:S(2)}, u32[]{:S(2)}) %collective-permute-start.20) | collective-permute-done | bytes 98336 | tf_op jit(solution)/shard_map/ppermute | solution.py:621
  66.6 4.3 %collective-permute-start.22 = (bf16[12,32,128]{2,1,0:T(8,128)(2,1)S(1)}, bf16[12,32,128]{2,1,0:T(8,128)(2,1)S(1)}, u32[]{:S(2)}, u32[]{:S(2)}) collective-permute-start(bf16[12,32,128]{2,1,0:T(8,128)(2,1)S(1)} %get-tuple-element.85.b_ref), channel_id=1, source_target_pairs={{1,0},{2,1},{3,2},{4,3},{5,4},{6,5},{7,6},{0,7},{9,8},{10,9},{11,1... | collective-permute-start | bytes 294920 | tf_op jit(solution)/shard_map/ppermute | solution.py:93
  70.9 2.7 %collective-permute-done.23.a_ref = bf16[12,32,128]{2,1,0:T(8,128)(2,1)S(1)} collective-permute-done((bf16[12,32,128]{2,1,0:T(8,128)(2,1)S(1)}, bf16[12,32,128]{2,1,0:T(8,128)(2,1)S(1)}, u32[]{:S(2)}, u32[]{:S(2)}) %collective-permute-start.23) | collective-permute-done | bytes 98336 | tf_op jit(solution)/shard_map/ppermute | solution.py:93
  74.8 2.1 %collective-permute-start.25 = (bf16[12,32,128]{2,1,0:T(8,128)(2,1)S(1)}, bf16[12,32,128]{2,1,0:T(8,128)(2,1)S(1)}, u32[]{:S(2)}, u32[]{:S(2)}) collective-permute-start(bf16[12,32,128]{2,1,0:T(8,128)(2,1)S(1)} %get-tuple-element.88.b_ref), channel_id=1, source_target_pairs={{0,1},{1,2},{2,3},{3,4},{4,5},{5,6},{6,7},{7,0},{8,9},{9,10},{10,1... | collective-permute-start | bytes 294920 | tf_op jit(solution)/shard_map/ppermute | solution.py:93
  76.9 2.7 %collective-permute-start.24 = (bf16[12,32,128]{2,1,0:T(8,128)(2,1)S(1)}, bf16[12,32,128]{2,1,0:T(8,128)(2,1)S(1)}, u32[]{:S(2)}, u32[]{:S(2)}) collective-permute-start(bf16[12,32,128]{2,1,0:T(8,128)(2,1)S(1)} %get-tuple-element.88.b_ref), channel_id=1, source_target_pairs={{1,0},{2,1},{3,2},{4,3},{5,4},{6,5},{7,6},{0,7},{9,8},{10,9},{11,1... | collective-permute-start | bytes 294920 | tf_op jit(solution)/shard_map/ppermute | solution.py:93
  90.9 2.9 %collective-permute-start.30 = (bf16[12,8,128]{2,1,0:T(8,128)(2,1)S(1)}, bf16[12,8,128]{2,1,0:T(8,128)(2,1)S(1)}, u32[]{:S(2)}, u32[]{:S(2)}) collective-permute-start(bf16[12,8,128]{2,1,0:T(8,128)(2,1)S(1)} %get-tuple-element.99.b_ref), channel_id=1, source_target_pairs={{1,0},{2,1},{3,2},{4,3},{5,4},{6,5},{7,6},{0,7},{9,8},{10,9},{11,1... | collective-permute-start | bytes 73736 | tf_op jit(solution)/shard_map/ppermute | solution.py:93
  97.0 4.5 %collective-permute-start.32 = (bf16[12,8,128]{2,1,0:T(8,128)(2,1)S(1)}, bf16[12,8,128]{2,1,0:T(8,128)(2,1)S(1)}, u32[]{:S(2)}, u32[]{:S(2)}) collective-permute-start(bf16[12,8,128]{2,1,0:T(8,128)(2,1)S(1)} %get-tuple-element.102.b_ref), channel_id=1, source_target_pairs={{1,0},{2,1},{3,2},{4,3},{5,4},{6,5},{7,6},{0,7},{9,8},{10,9},{11,1... | collective-permute-start | bytes 73736 | tf_op jit(solution)/shard_map/ppermute | solution.py:93
  104.4 4.8 %collective-permute-start.34 = (bf16[12,8,128]{2,1,0:T(8,128)(2,1)S(1)}, bf16[12,8,128]{2,1,0:T(8,128)(2,1)S(1)}, u32[]{:S(2)}, u32[]{:S(2)}) collective-permute-start(bf16[12,8,128]{2,1,0:T(8,128)(2,1)S(1)} %get-tuple-element.104.b_ref), channel_id=1, source_target_pairs={{1,0},{2,1},{3,2},{4,3},{5,4},{6,5},{7,6},{0,7},{9,8},{10,9},{11,1... | collective-permute-start | bytes 73736 | tf_op jit(solution)/shard_map/ppermute | solution.py:93
  112.2 4.8 %collective-permute-start.36 = (bf16[12,8,128]{2,1,0:T(8,128)(2,1)S(1)}, bf16[12,8,128]{2,1,0:T(8,128)(2,1)S(1)}, u32[]{:S(2)}, u32[]{:S(2)}) collective-permute-start(bf16[12,8,128]{2,1,0:T(8,128)(2,1)S(1)} %get-tuple-element.106.b_ref), channel_id=1, source_target_pairs={{1,0},{2,1},{3,2},{4,3},{5,4},{6,5},{7,6},{0,7},{9,8},{10,9},{11,1... | collective-permute-start | bytes 73736 | tf_op jit(solution)/shard_map/ppermute | solution.py:93
  119.9 4.9 %collective-permute-start.38 = (bf16[12,8,128]{2,1,0:T(8,128)(2,1)S(1)}, bf16[12,8,128]{2,1,0:T(8,128)(2,1)S(1)}, u32[]{:S(2)}, u32[]{:S(2)}) collective-permute-start(bf16[12,8,128]{2,1,0:T(8,128)(2,1)S(1)} %get-tuple-element.108.b_ref), channel_id=1, source_target_pairs={{1,0},{2,1},{3,2},{4,3},{5,4},{6,5},{7,6},{0,7},{9,8},{10,9},{11,1... | collective-permute-start | bytes 73736 | tf_op jit(solution)/shard_map/ppermute | solution.py:93
  127.8 4.8 %collective-permute-start.40 = (bf16[12,8,128]{2,1,0:T(8,128)(2,1)S(1)}, bf16[12,8,128]{2,1,0:T(8,128)(2,1)S(1)}, u32[]{:S(2)}, u32[]{:S(2)}) collective-permute-start(bf16[12,8,128]{2,1,0:T(8,128)(2,1)S(1)} %get-tuple-element.110.b_ref), channel_id=1, source_target_pairs={{1,0},{2,1},{3,2},{4,3},{5,4},{6,5},{7,6},{0,7},{9,8},{10,9},{11,1... | collective-permute-start | bytes 73736 | tf_op jit(solution)/shard_map/ppermute | solution.py:93
  135.7 4.8 %collective-permute-start.42 = (bf16[12,8,128]{2,1,0:T(8,128)(2,1)S(1)}, bf16[12,8,128]{2,1,0:T(8,128)(2,1)S(1)}, u32[]{:S(2)}, u32[]{:S(2)}) collective-permute-start(bf16[12,8,128]{2,1,0:T(8,128)(2,1)S(1)} %get-tuple-element.112.b_ref), channel_id=1, source_target_pairs={{1,0},{2,1},{3,2},{4,3},{5,4},{6,5},{7,6},{0,7},{9,8},{10,9},{11,1... | collective-permute-start | bytes 73736 | tf_op jit(solution)/shard_map/ppermute | solution.py:93
  145.0 2.4 %collective-permute-done.45.refs_2_ = bf16[12,8,128]{2,1,0:T(8,128)(2,1)S(1)} collective-permute-done((bf16[12,8,128]{2,1,0:T(8,128)(2,1)S(1)}, bf16[12,8,128]{2,1,0:T(8,128)(2,1)S(1)}, u32[]{:S(2)}, u32[]{:S(2)}) %collective-permute-start.45) | collective-permute-done | bytes 24608 | tf_op jit(solution)/shard_map/ppermute | solution.py:640
  148.7 4.8 %collective-permute-start.47 = (bf16[12,32,128]{2,1,0:T(8,128)(2,1)S(1)}, bf16[12,32,128]{2,1,0:T(8,128)(2,1)S(1)}, u32[]{:S(2)}, u32[]{:S(2)}) collective-permute-start(bf16[12,32,128]{2,1,0:T(8,128)(2,1)S(1)} %get-tuple-element.115.b_ref), channel_id=1, source_target_pairs={{1,0},{2,1},{3,2},{4,3},{5,4},{6,5},{7,6},{0,7},{9,8},{10,9},{11,1... | collective-permute-start | bytes 294920 | tf_op jit(solution)/shard_map/ppermute | solution.py:93
  153.5 2.5 %collective-permute-done.48.a_ref = bf16[12,32,128]{2,1,0:T(8,128)(2,1)S(1)} collective-permute-done((bf16[12,32,128]{2,1,0:T(8,128)(2,1)S(1)}, bf16[12,32,128]{2,1,0:T(8,128)(2,1)S(1)}, u32[]{:S(2)}, u32[]{:S(2)}) %collective-permute-start.48) | collective-permute-done | bytes 98336 | tf_op jit(solution)/shard_map/ppermute | solution.py:93
  157.3 3.1 %collective-permute-start.51 = (bf16[12,32,128]{2,1,0:T(8,128)(2,1)S(1)}, bf16[12,32,128]{2,1,0:T(8,128)(2,1)S(1)}, u32[]{:S(2)}, u32[]{:S(2)}) collective-permute-start(bf16[12,32,128]{2,1,0:T(8,128)(2,1)S(1)} %get-tuple-element.117.refs_7_), channel_id=1, source_target_pairs={{0,4},{1,5},{2,6},{3,7},{4,0},{5,1},{6,2},{7,3},{8,12},{9,13},{10,... | collective-permute-start | bytes 294920 | tf_op jit(solution)/shard_map/ppermute | solution.py:646
  161.1 2.1 %collective-permute-start.55 = (bf16[12,32,128]{2,1,0:T(8,128)(2,1)S(1)}, bf16[12,32,128]{2,1,0:T(8,128)(2,1)S(1)}, u32[]{:S(2)}, u32[]{:S(2)}) collective-permute-start(bf16[12,32,128]{2,1,0:T(8,128)(2,1)S(1)} %get-tuple-element.117.refs_7_), channel_id=1, source_target_pairs={{0,1},{1,0},{2,3},{3,2},{4,5},{5,4},{6,7},{7,6},{8,9},{9,8},{10,11... | collective-permute-start | bytes 294920 | tf_op jit(solution)/shard_map/ppermute | solution.py:98
  166.2 2.5 %collective-permute-start.52 = (bf16[12,32,128]{2,1,0:T(8,128)(2,1)S(1)}, bf16[12,32,128]{2,1,0:T(8,128)(2,1)S(1)}, u32[]{:S(2)}, u32[]{:S(2)}) collective-permute-start(bf16[12,32,128]{2,1,0:T(8,128)(2,1)S(1)} %collective-permute-done.51.refs_5_), channel_id=1, source_target_pairs={{0,1},{1,0},{2,3},{3,2},{4,5},{5,4},{6,7},{7,6},{8,9},{9,8},{10,11... | collective-permute-start | bytes 294920 | tf_op jit(solution)/shard_map/ppermute | solution.py:98
  169.4 2.4 %collective-permute-done.52.refs_1_ = bf16[12,32,128]{2,1,0:T(8,128)(2,1)S(1)} collective-permute-done((bf16[12,32,128]{2,1,0:T(8,128)(2,1)S(1)}, bf16[12,32,128]{2,1,0:T(8,128)(2,1)S(1)}, u32[]{:S(2)}, u32[]{:S(2)}) %collective-permute-start.52) | collective-permute-done | bytes 98336 | tf_op jit(solution)/shard_map/ppermute | solution.py:98
  173.3 6.0 %shard_map.181 = (f32[48,32,128]{2,1,0:T(8,128)}, f32[12,32,128]{2,1,0:T(8,128)}, f32[12,32,128]{2,1,0:T(8,128)}) custom-call(s32[5,48]{1,0:T(8,128)S(1)} %bitcast.14, s32[48]{0:T(128)S(1)} %copy-done.14, s32[49,128]{1,0:T(8,128)S(1)} %collective-permute-done.17.near_to_ref.near_ref, s32[49,128]{1,0:T(8,128)S(1)} %collective-permute-done.29.far_to_ref.far_ref, ...), custom_call_target="tpu_custom_call" | custom-call | bytes 28800000 | tf_op jit(solution)/shard_map/pallas_call | solution.py:401
  (137 shorter events, 72.2 us)
Async XLA Ops:
  7.6 7.4 %collective-permute-start.3 = (bf16[12,32,128]{2,1,0:T(8,128)(2,1)S(1)}, bf16[12,32,128]{2,1,0:T(8,128)(2,1)S(1)}, u32[]{:S(2)}, u32[]{:S(2)}) collective-permute-start(bf16[12,32,128]{2,1,0:T(8,128)(2,1)S(1)} %get-tuple-element.66.refs_3_), channel_id=1, source_target_pairs={{0,1},{1,0},{2,3},{3,2},{4,5},{5,4},{6,7},{7,6},{8,9},{9,8},{10,11... | collective-permute-start | bytes 294920 | tf_op jit(solution)/shard_map/ppermute | solution.py:98
  9.6 7.2 %collective-permute-start.1 = (bf16[12,32,128]{2,1,0:T(8,128)(2,1)S(1)}, bf16[12,32,128]{2,1,0:T(8,128)(2,1)S(1)}, u32[]{:S(2)}, u32[]{:S(2)}) collective-permute-start(bf16[12,32,128]{2,1,0:T(8,128)(2,1)S(1)} %get-tuple-element.64.refs_1_), channel_id=1, source_target_pairs={{0,1},{1,0},{2,3},{3,2},{4,5},{5,4},{6,7},{7,6},{8,9},{9,8},{10,11... | collective-permute-start | bytes 294920 | tf_op jit(solution)/shard_map/ppermute | solution.py:98
  10.1 8.3 %collective-permute-start.4 = (bf16[12,32,128]{2,1,0:T(8,128)(2,1)S(1)}, bf16[12,32,128]{2,1,0:T(8,128)(2,1)S(1)}, u32[]{:S(2)}, u32[]{:S(2)}) collective-permute-start(bf16[12,32,128]{2,1,0:T(8,128)(2,1)S(1)} %collective-permute-done.refs_4_), channel_id=1, source_target_pairs={{0,2},{1,7},{2,4},{3,1},{4,6},{5,3},{6,0},{7,5},{8,10},{9,15},{10,... | collective-permute-start | bytes 294920 | tf_op jit(solution)/shard_map/ppermute | solution.py:103
  13.3 10.9 %collective-permute-start.6 = (bf16[12,32,128]{2,1,0:T(8,128)(2,1)S(1)}, bf16[12,32,128]{2,1,0:T(8,128)(2,1)S(1)}, u32[]{:S(2)}, u32[]{:S(2)}) collective-permute-start(bf16[12,32,128]{2,1,0:T(8,128)(2,1)S(1)} %collective-permute-done.2.refs_6_), channel_id=1, source_target_pairs={{0,2},{1,7},{2,4},{3,1},{4,6},{5,3},{6,0},{7,5},{8,10},{9,15},{10,... | collective-permute-start | bytes 294920 | tf_op jit(solution)/shard_map/ppermute | solution.py:103
  15.0 9.2 %collective-permute-start.7 = (bf16[12,32,128]{2,1,0:T(8,128)(2,1)S(1)}, bf16[12,32,128]{2,1,0:T(8,128)(2,1)S(1)}, u32[]{:S(2)}, u32[]{:S(2)}) collective-permute-start(bf16[12,32,128]{2,1,0:T(8,128)(2,1)S(1)} %collective-permute-done.3.refs_7_), channel_id=1, source_target_pairs={{0,2},{1,7},{2,4},{3,1},{4,6},{5,3},{6,0},{7,5},{8,10},{9,15},{10,... | collective-permute-start | bytes 294920 | tf_op jit(solution)/shard_map/ppermute | solution.py:103
  16.8 7.4 %collective-permute-start.5 = (bf16[12,32,128]{2,1,0:T(8,128)(2,1)S(1)}, bf16[12,32,128]{2,1,0:T(8,128)(2,1)S(1)}, u32[]{:S(2)}, u32[]{:S(2)}) collective-permute-start(bf16[12,32,128]{2,1,0:T(8,128)(2,1)S(1)} %collective-permute-done.1.refs_5_), channel_id=1, source_target_pairs={{0,2},{1,7},{2,4},{3,1},{4,6},{5,3},{6,0},{7,5},{8,10},{9,15},{10,... | collective-permute-start | bytes 294920 | tf_op jit(solution)/shard_map/ppermute | solution.py:103
  27.0 7.9 %collective-permute-start.10 = (bf16[12,32,128]{2,1,0:T(8,128)(2,1)S(1)}, bf16[12,32,128]{2,1,0:T(8,128)(2,1)S(1)}, u32[]{:S(2)}, u32[]{:S(2)}) collective-permute-start(bf16[12,32,128]{2,1,0:T(8,128)(2,1)S(1)} %get-tuple-element.71.refs_2_), channel_id=1, source_target_pairs={{0,1},{1,0},{2,3},{3,2},{4,5},{5,4},{6,7},{7,6},{8,9},{9,8},{10,11... | collective-permute-start | bytes 294920 | tf_op jit(solution)/shard_map/ppermute | solution.py:98
  34.9 10.6 %collective-permute-start.14 = (bf16[12,32,128]{2,1,0:T(8,128)(2,1)S(1)}, bf16[12,32,128]{2,1,0:T(8,128)(2,1)S(1)}, u32[]{:S(2)}, u32[]{:S(2)}) collective-permute-start(bf16[12,32,128]{2,1,0:T(8,128)(2,1)S(1)} %collective-permute-done.10.refs_6_), channel_id=1, source_target_pairs={{0,2},{1,7},{2,4},{3,1},{4,6},{5,3},{6,0},{7,5},{8,10},{9,15},{10,... | collective-permute-start | bytes 294920 | tf_op jit(solution)/shard_map/ppermute | solution.py:103
  35.9 9.6 %collective-permute-start.15 = (bf16[12,32,128]{2,1,0:T(8,128)(2,1)S(1)}, bf16[12,32,128]{2,1,0:T(8,128)(2,1)S(1)}, u32[]{:S(2)}, u32[]{:S(2)}) collective-permute-start(bf16[12,32,128]{2,1,0:T(8,128)(2,1)S(1)} %collective-permute-done.11.after_ref.refs_7_), channel_id=1, source_target_pairs={{0,2},{1,7},{2,4},{3,1},{4,6},{5,3},{6,0},{7,5},{8,10},{9,15},{10,... | collective-permute-start | bytes 294920 | tf_op jit(solution)/shard_map/ppermute | solution.py:103
  37.8 7.7 %collective-permute-start.12 = (bf16[12,32,128]{2,1,0:T(8,128)(2,1)S(1)}, bf16[12,32,128]{2,1,0:T(8,128)(2,1)S(1)}, u32[]{:S(2)}, u32[]{:S(2)}) collective-permute-start(bf16[12,32,128]{2,1,0:T(8,128)(2,1)S(1)} %collective-permute-done.8.refs_4_), channel_id=1, source_target_pairs={{0,2},{1,7},{2,4},{3,1},{4,6},{5,3},{6,0},{7,5},{8,10},{9,15},{10,... | collective-permute-start | bytes 294920 | tf_op jit(solution)/shard_map/ppermute | solution.py:103
  39.4 6.8 %collective-permute-start.13 = (bf16[12,32,128]{2,1,0:T(8,128)(2,1)S(1)}, bf16[12,32,128]{2,1,0:T(8,128)(2,1)S(1)}, u32[]{:S(2)}, u32[]{:S(2)}) collective-permute-start(bf16[12,32,128]{2,1,0:T(8,128)(2,1)S(1)} %collective-permute-done.9.refs_5_), channel_id=1, source_target_pairs={{0,2},{1,7},{2,4},{3,1},{4,6},{5,3},{6,0},{7,5},{8,10},{9,15},{10,... | collective-permute-start | bytes 294920 | tf_op jit(solution)/shard_map/ppermute | solution.py:103
  50.2 7.0 %collective-permute-start.18 = (bf16[24,32,128]{2,1,0:T(8,128)(2,1)S(1)}, bf16[24,32,128]{2,1,0:T(8,128)(2,1)S(1)}, u32[]{:S(2)}, u32[]{:S(2)}) collective-permute-start(bf16[24,32,128]{2,1,0:T(8,128)(2,1)S(1)} %get-tuple-element.79), channel_id=1, source_target_pairs={{0,1},{1,0},{2,3},{3,2},{4,5},{5,4},{6,7},{7,6},{8,9},{9,8},{10,11... | collective-permute-start | bytes 589832 | tf_op jit(solution)/shard_map/ppermute | solution.py:98
  51.0 8.6 %collective-permute-start.16 = (bf16[24,32,128]{2,1,0:T(8,128)(2,1)S(1)}, bf16[24,32,128]{2,1,0:T(8,128)(2,1)S(1)}, u32[]{:S(2)}, u32[]{:S(2)}) collective-permute-start(bf16[24,32,128]{2,1,0:T(8,128)(2,1)S(1)} %get-tuple-element.73.after_ref), channel_id=1, source_target_pairs={{0,1},{1,0},{2,3},{3,2},{4,5},{5,4},{6,7},{7,6},{8,9},{9,8},{10,11... | collective-permute-start | bytes 589832 | tf_op jit(solution)/shard_map/ppermute | solution.py:98
  52.3 7.3 %collective-permute-start.17 = (s32[49,128]{1,0:T(8,128)S(1)}, s32[49,128]{1,0:T(8,128)S(1)}, u32[]{:S(2)}, u32[]{:S(2)}) collective-permute-start(s32[49,128]{1,0:T(8,128)S(1)} %get-tuple-element.74), channel_id=1, source_target_pairs={{0,1},{1,0},{2,3},{3,2},{4,5},{5,4},{6,7},{7,6},{8,9},{9,8},{10,11... | collective-permute-start | bytes 75272 | tf_op jit(solution)/shard_map/ppermute | solution.py:98
  66.1 7.5 %collective-permute-start.23 = (bf16[12,32,128]{2,1,0:T(8,128)(2,1)S(1)}, bf16[12,32,128]{2,1,0:T(8,128)(2,1)S(1)}, u32[]{:S(2)}, u32[]{:S(2)}) collective-permute-start(bf16[12,32,128]{2,1,0:T(8,128)(2,1)S(1)} %get-tuple-element.85.b_ref), channel_id=1, source_target_pairs={{0,1},{1,2},{2,3},{3,4},{4,5},{5,6},{6,7},{7,0},{8,9},{9,10},{10,1... | collective-permute-start | bytes 294920 | tf_op jit(solution)/shard_map/ppermute | solution.py:93
  66.6 7.0 %collective-permute-start.22 = (bf16[12,32,128]{2,1,0:T(8,128)(2,1)S(1)}, bf16[12,32,128]{2,1,0:T(8,128)(2,1)S(1)}, u32[]{:S(2)}, u32[]{:S(2)}) collective-permute-start(bf16[12,32,128]{2,1,0:T(8,128)(2,1)S(1)} %get-tuple-element.85.b_ref), channel_id=1, source_target_pairs={{1,0},{2,1},{3,2},{4,3},{5,4},{6,5},{7,6},{0,7},{9,8},{10,9},{11,1... | collective-permute-start | bytes 294920 | tf_op jit(solution)/shard_map/ppermute | solution.py:93
  74.8 7.5 %collective-permute-start.25 = (bf16[12,32,128]{2,1,0:T(8,128)(2,1)S(1)}, bf16[12,32,128]{2,1,0:T(8,128)(2,1)S(1)}, u32[]{:S(2)}, u32[]{:S(2)}) collective-permute-start(bf16[12,32,128]{2,1,0:T(8,128)(2,1)S(1)} %get-tuple-element.88.b_ref), channel_id=1, source_target_pairs={{0,1},{1,2},{2,3},{3,4},{4,5},{5,6},{6,7},{7,0},{8,9},{9,10},{10,1... | collective-permute-start | bytes 294920 | tf_op jit(solution)/shard_map/ppermute | solution.py:93
  79.6 7.6 %collective-permute-start.29 = (s32[49,128]{1,0:T(8,128)S(1)}, s32[49,128]{1,0:T(8,128)S(1)}, u32[]{:S(2)}, u32[]{:S(2)}) collective-permute-start(s32[49,128]{1,0:T(8,128)S(1)} %collective-permute-done.17.near_to_ref.near_ref), channel_id=1, source_target_pairs={{0,2},{1,7},{2,4},{3,1},{4,6},{5,3},{6,0},{7,5},{8,10},{9,15},{10,... | collective-permute-start | bytes 75272 | tf_op jit(solution)/shard_map/ppermute | solution.py:103
  104.4 6.6 %collective-permute-start.35 = (bf16[12,8,128]{2,1,0:T(8,128)(2,1)S(1)}, bf16[12,8,128]{2,1,0:T(8,128)(2,1)S(1)}, u32[]{:S(2)}, u32[]{:S(2)}) collective-permute-start(bf16[12,8,128]{2,1,0:T(8,128)(2,1)S(1)} %get-tuple-element.104.b_ref), channel_id=1, source_target_pairs={{0,1},{1,2},{2,3},{3,4},{4,5},{5,6},{6,7},{7,0},{8,9},{9,10},{10,1... | collective-permute-start | bytes 73736 | tf_op jit(solution)/shard_map/ppermute | solution.py:93
  104.4 6.6 %collective-permute-start.34 = (bf16[12,8,128]{2,1,0:T(8,128)(2,1)S(1)}, bf16[12,8,128]{2,1,0:T(8,128)(2,1)S(1)}, u32[]{:S(2)}, u32[]{:S(2)}) collective-permute-start(bf16[12,8,128]{2,1,0:T(8,128)(2,1)S(1)} %get-tuple-element.104.b_ref), channel_id=1, source_target_pairs={{1,0},{2,1},{3,2},{4,3},{5,4},{6,5},{7,6},{0,7},{9,8},{10,9},{11,1... | collective-permute-start | bytes 73736 | tf_op jit(solution)/shard_map/ppermute | solution.py:93
  112.1 6.6 %collective-permute-start.37 = (bf16[12,8,128]{2,1,0:T(8,128)(2,1)S(1)}, bf16[12,8,128]{2,1,0:T(8,128)(2,1)S(1)}, u32[]{:S(2)}, u32[]{:S(2)}) collective-permute-start(bf16[12,8,128]{2,1,0:T(8,128)(2,1)S(1)} %get-tuple-element.106.b_ref), channel_id=1, source_target_pairs={{0,1},{1,2},{2,3},{3,4},{4,5},{5,6},{6,7},{7,0},{8,9},{9,10},{10,1... | collective-permute-start | bytes 73736 | tf_op jit(solution)/shard_map/ppermute | solution.py:93
  112.2 6.6 %collective-permute-start.36 = (bf16[12,8,128]{2,1,0:T(8,128)(2,1)S(1)}, bf16[12,8,128]{2,1,0:T(8,128)(2,1)S(1)}, u32[]{:S(2)}, u32[]{:S(2)}) collective-permute-start(bf16[12,8,128]{2,1,0:T(8,128)(2,1)S(1)} %get-tuple-element.106.b_ref), channel_id=1, source_target_pairs={{1,0},{2,1},{3,2},{4,3},{5,4},{6,5},{7,6},{0,7},{9,8},{10,9},{11,1... | collective-permute-start | bytes 73736 | tf_op jit(solution)/shard_map/ppermute | solution.py:93
  119.9 6.7 %collective-permute-start.39 = (bf16[12,8,128]{2,1,0:T(8,128)(2,1)S(1)}, bf16[12,8,128]{2,1,0:T(8,128)(2,1)S(1)}, u32[]{:S(2)}, u32[]{:S(2)}) collective-permute-start(bf16[12,8,128]{2,1,0:T(8,128)(2,1)S(1)} %get-tuple-element.108.b_ref), channel_id=1, source_target_pairs={{0,1},{1,2},{2,3},{3,4},{4,5},{5,6},{6,7},{7,0},{8,9},{9,10},{10,1... | collective-permute-start | bytes 73736 | tf_op jit(solution)/shard_map/ppermute | solution.py:93
  119.9 6.6 %collective-permute-start.38 = (bf16[12,8,128]{2,1,0:T(8,128)(2,1)S(1)}, bf16[12,8,128]{2,1,0:T(8,128)(2,1)S(1)}, u32[]{:S(2)}, u32[]{:S(2)}) collective-permute-start(bf16[12,8,128]{2,1,0:T(8,128)(2,1)S(1)} %get-tuple-element.108.b_ref), channel_id=1, source_target_pairs={{1,0},{2,1},{3,2},{4,3},{5,4},{6,5},{7,6},{0,7},{9,8},{10,9},{11,1... | collective-permute-start | bytes 73736 | tf_op jit(solution)/shard_map/ppermute | solution.py:93
  127.7 6.6 %collective-permute-start.41 = (bf16[12,8,128]{2,1,0:T(8,128)(2,1)S(1)}, bf16[12,8,128]{2,1,0:T(8,128)(2,1)S(1)}, u32[]{:S(2)}, u32[]{:S(2)}) collective-permute-start(bf16[12,8,128]{2,1,0:T(8,128)(2,1)S(1)} %get-tuple-element.110.b_ref), channel_id=1, source_target_pairs={{0,1},{1,2},{2,3},{3,4},{4,5},{5,6},{6,7},{7,0},{8,9},{9,10},{10,1... | collective-permute-start | bytes 73736 | tf_op jit(solution)/shard_map/ppermute | solution.py:93
  135.5 6.8 %collective-permute-start.43 = (bf16[12,8,128]{2,1,0:T(8,128)(2,1)S(1)}, bf16[12,8,128]{2,1,0:T(8,128)(2,1)S(1)}, u32[]{:S(2)}, u32[]{:S(2)}) collective-permute-start(bf16[12,8,128]{2,1,0:T(8,128)(2,1)S(1)} %get-tuple-element.112.b_ref), channel_id=1, source_target_pairs={{0,1},{1,2},{2,3},{3,4},{4,5},{5,6},{6,7},{7,0},{8,9},{9,10},{10,1... | collective-permute-start | bytes 73736 | tf_op jit(solution)/shard_map/ppermute | solution.py:93
  148.6 7.4 %collective-permute-start.48 = (bf16[12,32,128]{2,1,0:T(8,128)(2,1)S(1)}, bf16[12,32,128]{2,1,0:T(8,128)(2,1)S(1)}, u32[]{:S(2)}, u32[]{:S(2)}) collective-permute-start(bf16[12,32,128]{2,1,0:T(8,128)(2,1)S(1)} %get-tuple-element.115.b_ref), channel_id=1, source_target_pairs={{0,1},{1,2},{2,3},{3,4},{4,5},{5,6},{6,7},{7,0},{8,9},{9,10},{10,1... | collective-permute-start | bytes 294920 | tf_op jit(solution)/shard_map/ppermute | solution.py:93
  148.7 7.4 %collective-permute-start.47 = (bf16[12,32,128]{2,1,0:T(8,128)(2,1)S(1)}, bf16[12,32,128]{2,1,0:T(8,128)(2,1)S(1)}, u32[]{:S(2)}, u32[]{:S(2)}) collective-permute-start(bf16[12,32,128]{2,1,0:T(8,128)(2,1)S(1)} %get-tuple-element.115.b_ref), channel_id=1, source_target_pairs={{1,0},{2,1},{3,2},{4,3},{5,4},{6,5},{7,6},{0,7},{9,8},{10,9},{11,1... | collective-permute-start | bytes 294920 | tf_op jit(solution)/shard_map/ppermute | solution.py:93
  157.2 6.8 %collective-permute-start.53 = (bf16[12,32,128]{2,1,0:T(8,128)(2,1)S(1)}, bf16[12,32,128]{2,1,0:T(8,128)(2,1)S(1)}, u32[]{:S(2)}, u32[]{:S(2)}) collective-permute-start(bf16[12,32,128]{2,1,0:T(8,128)(2,1)S(1)} %get-tuple-element.117.refs_7_), channel_id=1, source_target_pairs={{0,2},{1,3},{2,4},{3,5},{4,6},{5,7},{6,0},{7,1},{8,10},{9,11},{10,... | collective-permute-start | bytes 294920 | tf_op jit(solution)/shard_map/ppermute | solution.py:646
  157.3 8.9 %collective-permute-start.51 = (bf16[12,32,128]{2,1,0:T(8,128)(2,1)S(1)}, bf16[12,32,128]{2,1,0:T(8,128)(2,1)S(1)}, u32[]{:S(2)}, u32[]{:S(2)}) collective-permute-start(bf16[12,32,128]{2,1,0:T(8,128)(2,1)S(1)} %get-tuple-element.117.refs_7_), channel_id=1, source_target_pairs={{0,4},{1,5},{2,6},{3,7},{4,0},{5,1},{6,2},{7,3},{8,12},{9,13},{10,... | collective-permute-start | bytes 294920 | tf_op jit(solution)/shard_map/ppermute | solution.py:646
  160.4 8.3 %collective-permute-start.49 = (bf16[12,32,128]{2,1,0:T(8,128)(2,1)S(1)}, bf16[12,32,128]{2,1,0:T(8,128)(2,1)S(1)}, u32[]{:S(2)}, u32[]{:S(2)}) collective-permute-start(bf16[12,32,128]{2,1,0:T(8,128)(2,1)S(1)} %get-tuple-element.117.refs_7_), channel_id=1, source_target_pairs={{0,6},{1,7},{2,0},{3,1},{4,2},{5,3},{6,4},{7,5},{8,14},{9,15},{10,... | collective-permute-start | bytes 294920 | tf_op jit(solution)/shard_map/ppermute | solution.py:646
  161.1 7.7 %collective-permute-start.55 = (bf16[12,32,128]{2,1,0:T(8,128)(2,1)S(1)}, bf16[12,32,128]{2,1,0:T(8,128)(2,1)S(1)}, u32[]{:S(2)}, u32[]{:S(2)}) collective-permute-start(bf16[12,32,128]{2,1,0:T(8,128)(2,1)S(1)} %get-tuple-element.117.refs_7_), channel_id=1, source_target_pairs={{0,1},{1,0},{2,3},{3,2},{4,5},{5,4},{6,7},{7,6},{8,9},{9,8},{10,11... | collective-permute-start | bytes 294920 | tf_op jit(solution)/shard_map/ppermute | solution.py:98
  (40 other events, 286.8 us)

commit v2 on v1

--- a/solution.py
+++ b/solution.py
@@ -6,6 +6,7 @@
 from jax.sharding import PartitionSpec as P
 
 COARSE = 8
+SPLIT = (False,)
 HALVES, CHUNKS = 2, 2
 F32 = jnp.float32
 BF16 = jnp.bfloat16
@@ -36,10 +37,10 @@
     return base + (blk - 1) * per, blks * per
 
 
-def picked(cols_ref, row, ring, x_ref):
+def picked(cols_ref, row, ring, x_ref, skip=0):
     first, total = ring
     blocks = []
-    for k in range(cols_ref.shape[0]):
+    for k in range(skip, cols_ref.shape[0]):
         place = cols_ref[k, row] - first
         place = jnp.where(place < 0, place + total, place)
         place = jnp.where(place >= total, place - total, place)
@@ -52,10 +53,10 @@
     return times(picked(cols_ref, row, ring, x_ref), t)
 
 
-def packed_product(cols_ref, row, ring, x_ref, pack_ref):
+def packed_product(cols_ref, row, ring, x_ref, pack_ref, skip=0):
     kt, vb = pack_ref.shape[1] - 1, pack_ref.shape[2]
-    t = pack_ref[row, :kt].reshape(kt * vb, vb)
-    x = picked(cols_ref, row, ring, x_ref)
+    t = pack_ref[row, skip:kt].reshape((kt - skip) * vb, vb)
+    x = picked(cols_ref, row, ring, x_ref, skip)
     return lax.dot_general(x, t, NN, preferred_element_type=F32)
 
 
@@ -475,16 +476,37 @@
     )(pack, *terms)
 
 
+def less_own(pack, rhs, x):
+    def kernel(pack_ref, rhs_ref, x_ref, z_ref):
+        own = x_ref[...].astype(F32)
+        for i in range(rhs.shape[0]):
+            z_ref[i] = rhs_ref[i] - lax.dot_general(
+                own[i].astype(BF16), pack_ref[i, 0], NN, preferred_element_type=F32
+            )
+
+    return pl.pallas_call(
+        kernel,
+        in_specs=[VMEM] * 3,
+        out_specs=VMEM,
+        out_shape=sds(rhs.shape, F32),
+        compiler_params=params(12),
+        cost_estimate=cost(0.3),
+    )(pack, rhs, x)
+
+
 def small_sweep(folded, cols, x3, pack, rhs, field, last=False):
     n, r, vb = rhs.shape
     pick = BF16 if r % 16 == 0 else F32
     kinds = [BF16] if last else [BF16, F32]
+    skip = 1 if folded in SPLIT else 0
+    if skip:
+        rhs = less_own(pack, rhs, x3[1])
 
     def kernel(cols_ref, c_ref, b_ref, a_ref, pack_ref, rhs_ref, v_ref, *refs):
         out_refs, x_ref = refs[:-1], refs[-1]
         fill(x_ref, (a_ref, b_ref, c_ref))
         ring = first_before(n, folded)
-        zs = [rhs_ref[i] - packed_product(cols_ref, i, ring, x_ref, pack_ref) for i in range(n)]
+        zs = [rhs_ref[i] - packed_product(cols_ref, i, ring, x_ref, pack_ref, skip) for i in range(n)]
         vs = [v_ref[i] + smoothed(zs[i], pack_ref, i) for i in range(n)]
         for i, v in enumerate(vs):
             for out_ref in out_refs:

time: 180 us -> 179 us (level)
  transfers between devices with their start and end apart: 56 -> 56, of which waited for: 32 -> 32; matrix products, arithmetic and copies ran while one was open for 0% -> 0% of each run, Pallas kernels for 8% -> 9%
where the time goes in v2:
time: 179 us
  starting transfers between devices  89.3 us (50%)
  waiting for transfers between devices  41.9 us (23%)
  Pallas kernels  40.6 us (23%)
  local copies, waits for them, and re-layouts  5.82 us (3%)
    ppermute x20, starting transfers between devices, halos(): return (lax.ppermute(value, 'blk', up), lax.ppermute(value, 'blk', down))  48.5 us
    ppermute x15, starting transfers between devices, partner(): return lax.ppermute(value, 'blk', [(i, i ^ 1) for i in range(n)])  19.5 us
    ppermute x20, waiting for transfers between devices, halos(): return (lax.ppermute(value, 'blk', up), lax.ppermute(value, 'blk', down))  18.2 us
    ppermute x15, waiting for transfers between devices, partner(): return lax.ppermute(value, 'blk', [(i, i ^ 1) for i in range(n)])  12.6 us
    ppermute x9, starting transfers between devices, forwarded(): lax.ppermute(value, 'blk', [(i, (i + 2 - 4 * (i % 2)) % n) for i in range...  11 us
    pallas_call x9, Pallas kernels, small_sweep(): pl.pallas_call(kernel, in_specs=[SMEM] + [VMEM] * 6, out_specs=[VMEM] * l...  9.67 us
    pallas_call x3, Pallas kernels, packed(): pl.pallas_call(kernel, in_specs=[VMEM] * 2 + [ANY], out_specs=VMEM, out_s...  7.57 us
    pallas_call x1, Pallas kernels, fine_last(): pl.pallas_call(kernel, in_specs=[SMEM] * 4 + [VMEM] * (5 + parts + len(fi...  6 us
  transfers between devices with their start and end apart: 56, of which 32 were waited for; matrix products, arithmetic and copies ran while one was open for 0% of the time, Pallas kernels for 9%

profile of v2, /device:TPU:0, one launch (start us, length us, event | category | flops | bytes accessed | tf_op | source)
XLA Modules:
  0.0 178.7 jit_solution(8954907388936509922)
XLA Ops:
  3.8 3.0 %collective-permute-start = (bf16[12,32,128]{2,1,0:T(8,128)(2,1)S(1)}, bf16[12,32,128]{2,1,0:T(8,128)(2,1)S(1)}, u32[]{:S(2)}, u32[]{:S(2)}) collective-permute-start(bf16[12,32,128]{2,1,0:T(8,128)(2,1)S(1)} %get-tuple-element.63.refs_0_), channel_id=1, source_target_pairs={{0,1},{1,0},{2,3},{3,2},{4,5},{5,4},{6,7},{7,6},{8,9},{9,8},{10,11... | collective-permute-start | bytes 294920 | tf_op jit(solution)/shard_map/ppermute | solution.py:99
  7.6 2.0 %collective-permute-start.3 = (bf16[12,32,128]{2,1,0:T(8,128)(2,1)S(1)}, bf16[12,32,128]{2,1,0:T(8,128)(2,1)S(1)}, u32[]{:S(2)}, u32[]{:S(2)}) collective-permute-start(bf16[12,32,128]{2,1,0:T(8,128)(2,1)S(1)} %get-tuple-element.66.refs_3_), channel_id=1, source_target_pairs={{0,1},{1,0},{2,3},{3,2},{4,5},{5,4},{6,7},{7,6},{8,9},{9,8},{10,11... | collective-permute-start | bytes 294920 | tf_op jit(solution)/shard_map/ppermute | solution.py:99
  18.4 3.2 %copy-done.4 = bf16[48,5,128,128]{3,2,1,0:T(8,128)(2,1)S(1)} copy-done((bf16[48,5,128,128]{3,2,1,0:T(8,128)(2,1)S(1)}, bf16[48,5,128,128]{3,2,1,0:T(8,128)(2,1)}, u32[]{:S(2)}) %copy-start.4) | copy-done | bytes 7864344
  21.6 2.6 %shard_map.159.refs_12_.t_ref = bf16[48,5,128,128]{3,2,1,0:T(8,128)(2,1)S(1)} custom-call(bf16[48,5,128,128]{3,2,1,0:T(8,128)(2,1)S(1)} %copy-done.4, bf16[12,32,128]{2,1,0:T(8,128)(2,1)S(1)} %collective-permute-done.4.after_ref.refs_8_), custom_call_target="tpu_custom_call" | custom-call | bytes 9000000 | tf_op jit(solution)/shard_map/pallas_call | solution.py:166
  24.3 2.7 %shard_map.161 = (f32[24,32,128]{2,1,0:T(8,128)S(1)}, bf16[12,32,128]{2,1,0:T(8,128)(2,1)S(1)}, bf16[12,32,128]{2,1,0:T(8,128)(2,1)S(1)}) custom-call(s32[5,48]{1,0:T(8,128)S(1)} %bitcast.11, bf16[12,32,128]{2,1,0:T(8,128)(2,1)S(1)} %get-tuple-element.63.refs_0_, bf16[12,32,128]{2,1,0:T(8,128)(2,1)S(1)} %get-tuple-element.64.refs_1_, ...), custom_call_target="tpu_custom_call" | custom-call | bytes 10799999 | tf_op jit(solution)/shard_map/pallas_call | solution.py:208
  27.0 3.0 %collective-permute-start.10 = (bf16[12,32,128]{2,1,0:T(8,128)(2,1)S(1)}, bf16[12,32,128]{2,1,0:T(8,128)(2,1)S(1)}, u32[]{:S(2)}, u32[]{:S(2)}) collective-permute-start(bf16[12,32,128]{2,1,0:T(8,128)(2,1)S(1)} %get-tuple-element.71.refs_2_), channel_id=1, source_target_pairs={{0,1},{1,0},{2,3},{3,2},{4,5},{5,4},{6,7},{7,6},{8,9},{9,8},{10,11... | collective-permute-start | bytes 294920 | tf_op jit(solution)/shard_map/ppermute | solution.py:99
  30.1 2.7 %shard_map.160 = (f32[24,32,128]{2,1,0:T(8,128)S(1)}, bf16[12,32,128]{2,1,0:T(8,128)(2,1)S(1)}, bf16[12,32,128]{2,1,0:T(8,128)(2,1)S(1)}) custom-call(s32[5,48]{1,0:T(8,128)S(1)} %bitcast.12, bf16[12,32,128]{2,1,0:T(8,128)(2,1)S(1)} %get-tuple-element.63.refs_0_, bf16[12,32,128]{2,1,0:T(8,128)(2,1)S(1)} %get-tuple-element.64.refs_1_, ...), custom_call_target="tpu_custom_call" | custom-call | bytes 10799999 | tf_op jit(solution)/shard_map/pallas_call | solution.py:208
  32.8 2.0 %collective-permute-start.8 = (bf16[12,32,128]{2,1,0:T(8,128)(2,1)S(1)}, bf16[12,32,128]{2,1,0:T(8,128)(2,1)S(1)}, u32[]{:S(2)}, u32[]{:S(2)}) collective-permute-start(bf16[12,32,128]{2,1,0:T(8,128)(2,1)S(1)} %get-tuple-element.68.refs_0_), channel_id=1, source_target_pairs={{0,1},{1,0},{2,3},{3,2},{4,5},{5,4},{6,7},{7,6},{8,9},{9,8},{10,11... | collective-permute-start | bytes 294920 | tf_op jit(solution)/shard_map/ppermute | solution.py:99
  40.4 5.0 %shard_map.162.refs_12_.refs_8_ = bf16[48,6,128,128]{3,2,1,0:T(8,128)(2,1)S(1)} custom-call(bf16[48,5,128,128]{3,2,1,0:T(8,128)(2,1)S(1)} %shard_map.159.refs_12_.t_ref, bf16[48,128,128]{2,1,0:T(8,128)(2,1)S(1)} %copy-done.1, bf16[12,32,128]{2,1,0:T(8,128)(2,1)S(1)} %collective-permute-done.11.after_ref.refs_7_), custom_call_target="tpu_custom_call" | custom-call | bytes 6000000 | tf_op jit(solution)/shard_map/pallas_call | solution.py:442
  46.2 3.9 %shard_map.163 = (f32[48,32,128]{2,1,0:T(8,128)S(1)}, f32[48,32,128]{2,1,0:T(8,128)S(1)}, bf16[24,32,128]{2,1,0:T(8,128)(2,1)S(1)}, bf16[24,32,128]{2,1,0:T(8,128)(2,1)S(1)}, s32[49,128]{1,0:T(8,128)S(1)}) custom-call(s32[5,48]{1,0:T(8,128)S(1)} %bitcast.13, s32[48]{0:T(128)S(1)} %copy-done.14, bf16[12,32,128]{2,1,0:T(8,128)(2,1)S(1)} %get-tuple-element.68.refs_0_, ...), custom_call_target="tpu_custom_call" | custom-call | bytes 21600000 | tf_op jit(solution)/shard_map/pallas_call | solution.py:280
  57.3 2.3 %collective-permute-done.17.near_to_ref.near_ref = s32[49,128]{1,0:T(8,128)S(1)} collective-permute-done((s32[49,128]{1,0:T(8,128)S(1)}, s32[49,128]{1,0:T(8,128)S(1)}, u32[]{:S(2)}, u32[]{:S(2)}) %collective-permute-start.17) | collective-permute-done | bytes 25120 | tf_op jit(solution)/shard_map/ppermute | solution.py:99
  61.6 2.1 %collective-permute-done.19.refs_1_ = bf16[12,32,128]{2,1,0:T(8,128)(2,1)S(1)} collective-permute-done((bf16[12,32,128]{2,1,0:T(8,128)(2,1)S(1)}, bf16[12,32,128]{2,1,0:T(8,128)(2,1)S(1)}, u32[]{:S(2)}, u32[]{:S(2)}) %collective-permute-start.19) | collective-permute-done | bytes 98336 | tf_op jit(solution)/shard_map/ppermute | solution.py:643
  63.7 2.2 %collective-permute-done.20.refs_2_ = bf16[12,32,128]{2,1,0:T(8,128)(2,1)S(1)} collective-permute-done((bf16[12,32,128]{2,1,0:T(8,128)(2,1)S(1)}, bf16[12,32,128]{2,1,0:T(8,128)(2,1)S(1)}, u32[]{:S(2)}, u32[]{:S(2)}) %collective-permute-start.20) | collective-permute-done | bytes 98336 | tf_op jit(solution)/shard_map/ppermute | solution.py:643
  66.6 4.3 %collective-permute-start.22 = (bf16[12,32,128]{2,1,0:T(8,128)(2,1)S(1)}, bf16[12,32,128]{2,1,0:T(8,128)(2,1)S(1)}, u32[]{:S(2)}, u32[]{:S(2)}) collective-permute-start(bf16[12,32,128]{2,1,0:T(8,128)(2,1)S(1)} %get-tuple-element.85.b_ref), channel_id=1, source_target_pairs={{1,0},{2,1},{3,2},{4,3},{5,4},{6,5},{7,6},{0,7},{9,8},{10,9},{11,1... | collective-permute-start | bytes 294920 | tf_op jit(solution)/shard_map/ppermute | solution.py:94
  70.9 2.7 %collective-permute-done.23.a_ref = bf16[12,32,128]{2,1,0:T(8,128)(2,1)S(1)} collective-permute-done((bf16[12,32,128]{2,1,0:T(8,128)(2,1)S(1)}, bf16[12,32,128]{2,1,0:T(8,128)(2,1)S(1)}, u32[]{:S(2)}, u32[]{:S(2)}) %collective-permute-start.23) | collective-permute-done | bytes 98336 | tf_op jit(solution)/shard_map/ppermute | solution.py:94
  74.8 2.1 %collective-permute-start.25 = (bf16[12,32,128]{2,1,0:T(8,128)(2,1)S(1)}, bf16[12,32,128]{2,1,0:T(8,128)(2,1)S(1)}, u32[]{:S(2)}, u32[]{:S(2)}) collective-permute-start(bf16[12,32,128]{2,1,0:T(8,128)(2,1)S(1)} %get-tuple-element.88.b_ref), channel_id=1, source_target_pairs={{0,1},{1,2},{2,3},{3,4},{4,5},{5,6},{6,7},{7,0},{8,9},{9,10},{10,1... | collective-permute-start | bytes 294920 | tf_op jit(solution)/shard_map/ppermute | solution.py:94
  76.9 2.7 %collective-permute-start.24 = (bf16[12,32,128]{2,1,0:T(8,128)(2,1)S(1)}, bf16[12,32,128]{2,1,0:T(8,128)(2,1)S(1)}, u32[]{:S(2)}, u32[]{:S(2)}) collective-permute-start(bf16[12,32,128]{2,1,0:T(8,128)(2,1)S(1)} %get-tuple-element.88.b_ref), channel_id=1, source_target_pairs={{1,0},{2,1},{3,2},{4,3},{5,4},{6,5},{7,6},{0,7},{9,8},{10,9},{11,1... | collective-permute-start | bytes 294920 | tf_op jit(solution)/shard_map/ppermute | solution.py:94
  90.9 2.9 %collective-permute-start.30 = (bf16[12,8,128]{2,1,0:T(8,128)(2,1)S(1)}, bf16[12,8,128]{2,1,0:T(8,128)(2,1)S(1)}, u32[]{:S(2)}, u32[]{:S(2)}) collective-permute-start(bf16[12,8,128]{2,1,0:T(8,128)(2,1)S(1)} %get-tuple-element.99.x_ref.b_ref), channel_id=1, source_target_pairs={{1,0},{2,1},{3,2},{4,3},{5,4},{6,5},{7,6},{0,7},{9,8},{10,9},{11,1... | collective-permute-start | bytes 73736 | tf_op jit(solution)/shard_map/ppermute | solution.py:94
  96.9 4.5 %collective-permute-start.32 = (bf16[12,8,128]{2,1,0:T(8,128)(2,1)S(1)}, bf16[12,8,128]{2,1,0:T(8,128)(2,1)S(1)}, u32[]{:S(2)}, u32[]{:S(2)}) collective-permute-start(bf16[12,8,128]{2,1,0:T(8,128)(2,1)S(1)} %get-tuple-element.102.x_ref.b_ref), channel_id=1, source_target_pairs={{1,0},{2,1},{3,2},{4,3},{5,4},{6,5},{7,6},{0,7},{9,8},{10,9},{11,1... | collective-permute-start | bytes 73736 | tf_op jit(solution)/shard_map/ppermute | solution.py:94
  104.2 4.8 %collective-permute-start.34 = (bf16[12,8,128]{2,1,0:T(8,128)(2,1)S(1)}, bf16[12,8,128]{2,1,0:T(8,128)(2,1)S(1)}, u32[]{:S(2)}, u32[]{:S(2)}) collective-permute-start(bf16[12,8,128]{2,1,0:T(8,128)(2,1)S(1)} %get-tuple-element.104.x_ref.b_ref), channel_id=1, source_target_pairs={{1,0},{2,1},{3,2},{4,3},{5,4},{6,5},{7,6},{0,7},{9,8},{10,9},{11,1... | collective-permute-start | bytes 73736 | tf_op jit(solution)/shard_map/ppermute | solution.py:94
  111.8 4.8 %collective-permute-start.36 = (bf16[12,8,128]{2,1,0:T(8,128)(2,1)S(1)}, bf16[12,8,128]{2,1,0:T(8,128)(2,1)S(1)}, u32[]{:S(2)}, u32[]{:S(2)}) collective-permute-start(bf16[12,8,128]{2,1,0:T(8,128)(2,1)S(1)} %get-tuple-element.106.x_ref.b_ref), channel_id=1, source_target_pairs={{1,0},{2,1},{3,2},{4,3},{5,4},{6,5},{7,6},{0,7},{9,8},{10,9},{11,1... | collective-permute-start | bytes 73736 | tf_op jit(solution)/shard_map/ppermute | solution.py:94
  119.5 4.8 %collective-permute-start.38 = (bf16[12,8,128]{2,1,0:T(8,128)(2,1)S(1)}, bf16[12,8,128]{2,1,0:T(8,128)(2,1)S(1)}, u32[]{:S(2)}, u32[]{:S(2)}) collective-permute-start(bf16[12,8,128]{2,1,0:T(8,128)(2,1)S(1)} %get-tuple-element.108.x_ref.b_ref), channel_id=1, source_target_pairs={{1,0},{2,1},{3,2},{4,3},{5,4},{6,5},{7,6},{0,7},{9,8},{10,9},{11,1... | collective-permute-start | bytes 73736 | tf_op jit(solution)/shard_map/ppermute | solution.py:94
  127.2 4.8 %collective-permute-start.40 = (bf16[12,8,128]{2,1,0:T(8,128)(2,1)S(1)}, bf16[12,8,128]{2,1,0:T(8,128)(2,1)S(1)}, u32[]{:S(2)}, u32[]{:S(2)}) collective-permute-start(bf16[12,8,128]{2,1,0:T(8,128)(2,1)S(1)} %get-tuple-element.110.x_ref.b_ref), channel_id=1, source_target_pairs={{1,0},{2,1},{3,2},{4,3},{5,4},{6,5},{7,6},{0,7},{9,8},{10,9},{11,1... | collective-permute-start | bytes 73736 | tf_op jit(solution)/shard_map/ppermute | solution.py:94
  135.0 4.8 %collective-permute-start.42 = (bf16[12,8,128]{2,1,0:T(8,128)(2,1)S(1)}, bf16[12,8,128]{2,1,0:T(8,128)(2,1)S(1)}, u32[]{:S(2)}, u32[]{:S(2)}) collective-permute-start(bf16[12,8,128]{2,1,0:T(8,128)(2,1)S(1)} %get-tuple-element.112.x_ref.b_ref), channel_id=1, source_target_pairs={{1,0},{2,1},{3,2},{4,3},{5,4},{6,5},{7,6},{0,7},{9,8},{10,9},{11,1... | collective-permute-start | bytes 73736 | tf_op jit(solution)/shard_map/ppermute | solution.py:94
  144.2 2.4 %collective-permute-done.45.refs_2_ = bf16[12,8,128]{2,1,0:T(8,128)(2,1)S(1)} collective-permute-done((bf16[12,8,128]{2,1,0:T(8,128)(2,1)S(1)}, bf16[12,8,128]{2,1,0:T(8,128)(2,1)S(1)}, u32[]{:S(2)}, u32[]{:S(2)}) %collective-permute-start.45) | collective-permute-done | bytes 24608 | tf_op jit(solution)/shard_map/ppermute | solution.py:662
  147.9 4.8 %collective-permute-start.47 = (bf16[12,32,128]{2,1,0:T(8,128)(2,1)S(1)}, bf16[12,32,128]{2,1,0:T(8,128)(2,1)S(1)}, u32[]{:S(2)}, u32[]{:S(2)}) collective-permute-start(bf16[12,32,128]{2,1,0:T(8,128)(2,1)S(1)} %get-tuple-element.115.b_ref), channel_id=1, source_target_pairs={{1,0},{2,1},{3,2},{4,3},{5,4},{6,5},{7,6},{0,7},{9,8},{10,9},{11,1... | collective-permute-start | bytes 294920 | tf_op jit(solution)/shard_map/ppermute | solution.py:94
  152.8 2.5 %collective-permute-done.48.a_ref = bf16[12,32,128]{2,1,0:T(8,128)(2,1)S(1)} collective-permute-done((bf16[12,32,128]{2,1,0:T(8,128)(2,1)S(1)}, bf16[12,32,128]{2,1,0:T(8,128)(2,1)S(1)}, u32[]{:S(2)}, u32[]{:S(2)}) %collective-permute-start.48) | collective-permute-done | bytes 98336 | tf_op jit(solution)/shard_map/ppermute | solution.py:94
  156.5 3.1 %collective-permute-start.51 = (bf16[12,32,128]{2,1,0:T(8,128)(2,1)S(1)}, bf16[12,32,128]{2,1,0:T(8,128)(2,1)S(1)}, u32[]{:S(2)}, u32[]{:S(2)}) collective-permute-start(bf16[12,32,128]{2,1,0:T(8,128)(2,1)S(1)} %get-tuple-element.117.refs_7_), channel_id=1, source_target_pairs={{0,4},{1,5},{2,6},{3,7},{4,0},{5,1},{6,2},{7,3},{8,12},{9,13},{10,... | collective-permute-start | bytes 294920 | tf_op jit(solution)/shard_map/ppermute | solution.py:668
  160.3 2.1 %collective-permute-start.55 = (bf16[12,32,128]{2,1,0:T(8,128)(2,1)S(1)}, bf16[12,32,128]{2,1,0:T(8,128)(2,1)S(1)}, u32[]{:S(2)}, u32[]{:S(2)}) collective-permute-start(bf16[12,32,128]{2,1,0:T(8,128)(2,1)S(1)} %get-tuple-element.117.refs_7_), channel_id=1, source_target_pairs={{0,1},{1,0},{2,3},{3,2},{4,5},{5,4},{6,7},{7,6},{8,9},{9,8},{10,11... | collective-permute-start | bytes 294920 | tf_op jit(solution)/shard_map/ppermute | solution.py:99
  165.5 2.4 %collective-permute-start.52 = (bf16[12,32,128]{2,1,0:T(8,128)(2,1)S(1)}, bf16[12,32,128]{2,1,0:T(8,128)(2,1)S(1)}, u32[]{:S(2)}, u32[]{:S(2)}) collective-permute-start(bf16[12,32,128]{2,1,0:T(8,128)(2,1)S(1)} %collective-permute-done.51.refs_5_), channel_id=1, source_target_pairs={{0,1},{1,0},{2,3},{3,2},{4,5},{5,4},{6,7},{7,6},{8,9},{9,8},{10,11... | collective-permute-start | bytes 294920 | tf_op jit(solution)/shard_map/ppermute | solution.py:99
  168.7 2.3 %collective-permute-done.52.refs_1_ = bf16[12,32,128]{2,1,0:T(8,128)(2,1)S(1)} collective-permute-done((bf16[12,32,128]{2,1,0:T(8,128)(2,1)S(1)}, bf16[12,32,128]{2,1,0:T(8,128)(2,1)S(1)}, u32[]{:S(2)}, u32[]{:S(2)}) %collective-permute-start.52) | collective-permute-done | bytes 98336 | tf_op jit(solution)/shard_map/ppermute | solution.py:99
  172.5 6.0 %shard_map.188 = (f32[48,32,128]{2,1,0:T(8,128)}, f32[12,32,128]{2,1,0:T(8,128)}, f32[12,32,128]{2,1,0:T(8,128)}) custom-call(s32[5,48]{1,0:T(8,128)S(1)} %bitcast.14, s32[48]{0:T(128)S(1)} %copy-done.14, s32[49,128]{1,0:T(8,128)S(1)} %collective-permute-done.17.near_to_ref.near_ref, s32[49,128]{1,0:T(8,128)S(1)} %collective-permute-done.29.far_to_ref.far_ref, ...), custom_call_target="tpu_custom_call" | custom-call | bytes 28800000 | tf_op jit(solution)/shard_map/pallas_call | solution.py:402
  (144 shorter events, 71.6 us)
Async XLA Ops:
  7.6 7.4 %collective-permute-start.3 = (bf16[12,32,128]{2,1,0:T(8,128)(2,1)S(1)}, bf16[12,32,128]{2,1,0:T(8,128)(2,1)S(1)}, u32[]{:S(2)}, u32[]{:S(2)}) collective-permute-start(bf16[12,32,128]{2,1,0:T(8,128)(2,1)S(1)} %get-tuple-element.66.refs_3_), channel_id=1, source_target_pairs={{0,1},{1,0},{2,3},{3,2},{4,5},{5,4},{6,7},{7,6},{8,9},{9,8},{10,11... | collective-permute-start | bytes 294920 | tf_op jit(solution)/shard_map/ppermute | solution.py:99
  9.6 7.2 %collective-permute-start.1 = (bf16[12,32,128]{2,1,0:T(8,128)(2,1)S(1)}, bf16[12,32,128]{2,1,0:T(8,128)(2,1)S(1)}, u32[]{:S(2)}, u32[]{:S(2)}) collective-permute-start(bf16[12,32,128]{2,1,0:T(8,128)(2,1)S(1)} %get-tuple-element.64.refs_1_), channel_id=1, source_target_pairs={{0,1},{1,0},{2,3},{3,2},{4,5},{5,4},{6,7},{7,6},{8,9},{9,8},{10,11... | collective-permute-start | bytes 294920 | tf_op jit(solution)/shard_map/ppermute | solution.py:99
  10.1 8.3 %collective-permute-start.4 = (bf16[12,32,128]{2,1,0:T(8,128)(2,1)S(1)}, bf16[12,32,128]{2,1,0:T(8,128)(2,1)S(1)}, u32[]{:S(2)}, u32[]{:S(2)}) collective-permute-start(bf16[12,32,128]{2,1,0:T(8,128)(2,1)S(1)} %collective-permute-done.refs_4_), channel_id=1, source_target_pairs={{0,2},{1,7},{2,4},{3,1},{4,6},{5,3},{6,0},{7,5},{8,10},{9,15},{10,... | collective-permute-start | bytes 294920 | tf_op jit(solution)/shard_map/ppermute | solution.py:104
  13.3 10.9 %collective-permute-start.6 = (bf16[12,32,128]{2,1,0:T(8,128)(2,1)S(1)}, bf16[12,32,128]{2,1,0:T(8,128)(2,1)S(1)}, u32[]{:S(2)}, u32[]{:S(2)}) collective-permute-start(bf16[12,32,128]{2,1,0:T(8,128)(2,1)S(1)} %collective-permute-done.2.refs_6_), channel_id=1, source_target_pairs={{0,2},{1,7},{2,4},{3,1},{4,6},{5,3},{6,0},{7,5},{8,10},{9,15},{10,... | collective-permute-start | bytes 294920 | tf_op jit(solution)/shard_map/ppermute | solution.py:104
  15.0 9.2 %collective-permute-start.7 = (bf16[12,32,128]{2,1,0:T(8,128)(2,1)S(1)}, bf16[12,32,128]{2,1,0:T(8,128)(2,1)S(1)}, u32[]{:S(2)}, u32[]{:S(2)}) collective-permute-start(bf16[12,32,128]{2,1,0:T(8,128)(2,1)S(1)} %collective-permute-done.3.refs_7_), channel_id=1, source_target_pairs={{0,2},{1,7},{2,4},{3,1},{4,6},{5,3},{6,0},{7,5},{8,10},{9,15},{10,... | collective-permute-start | bytes 294920 | tf_op jit(solution)/shard_map/ppermute | solution.py:104
  16.8 7.4 %collective-permute-start.5 = (bf16[12,32,128]{2,1,0:T(8,128)(2,1)S(1)}, bf16[12,32,128]{2,1,0:T(8,128)(2,1)S(1)}, u32[]{:S(2)}, u32[]{:S(2)}) collective-permute-start(bf16[12,32,128]{2,1,0:T(8,128)(2,1)S(1)} %collective-permute-done.1.refs_5_), channel_id=1, source_target_pairs={{0,2},{1,7},{2,4},{3,1},{4,6},{5,3},{6,0},{7,5},{8,10},{9,15},{10,... | collective-permute-start | bytes 294920 | tf_op jit(solution)/shard_map/ppermute | solution.py:104
  27.0 7.9 %collective-permute-start.10 = (bf16[12,32,128]{2,1,0:T(8,128)(2,1)S(1)}, bf16[12,32,128]{2,1,0:T(8,128)(2,1)S(1)}, u32[]{:S(2)}, u32[]{:S(2)}) collective-permute-start(bf16[12,32,128]{2,1,0:T(8,128)(2,1)S(1)} %get-tuple-element.71.refs_2_), channel_id=1, source_target_pairs={{0,1},{1,0},{2,3},{3,2},{4,5},{5,4},{6,7},{7,6},{8,9},{9,8},{10,11... | collective-permute-start | bytes 294920 | tf_op jit(solution)/shard_map/ppermute | solution.py:99
  34.9 10.6 %collective-permute-start.14 = (bf16[12,32,128]{2,1,0:T(8,128)(2,1)S(1)}, bf16[12,32,128]{2,1,0:T(8,128)(2,1)S(1)}, u32[]{:S(2)}, u32[]{:S(2)}) collective-permute-start(bf16[12,32,128]{2,1,0:T(8,128)(2,1)S(1)} %collective-permute-done.10.refs_6_), channel_id=1, source_target_pairs={{0,2},{1,7},{2,4},{3,1},{4,6},{5,3},{6,0},{7,5},{8,10},{9,15},{10,... | collective-permute-start | bytes 294920 | tf_op jit(solution)/shard_map/ppermute | solution.py:104
  35.9 9.6 %collective-permute-start.15 = (bf16[12,32,128]{2,1,0:T(8,128)(2,1)S(1)}, bf16[12,32,128]{2,1,0:T(8,128)(2,1)S(1)}, u32[]{:S(2)}, u32[]{:S(2)}) collective-permute-start(bf16[12,32,128]{2,1,0:T(8,128)(2,1)S(1)} %collective-permute-done.11.after_ref.refs_7_), channel_id=1, source_target_pairs={{0,2},{1,7},{2,4},{3,1},{4,6},{5,3},{6,0},{7,5},{8,10},{9,15},{10,... | collective-permute-start | bytes 294920 | tf_op jit(solution)/shard_map/ppermute | solution.py:104
  37.8 7.7 %collective-permute-start.12 = (bf16[12,32,128]{2,1,0:T(8,128)(2,1)S(1)}, bf16[12,32,128]{2,1,0:T(8,128)(2,1)S(1)}, u32[]{:S(2)}, u32[]{:S(2)}) collective-permute-start(bf16[12,32,128]{2,1,0:T(8,128)(2,1)S(1)} %collective-permute-done.8.refs_4_), channel_id=1, source_target_pairs={{0,2},{1,7},{2,4},{3,1},{4,6},{5,3},{6,0},{7,5},{8,10},{9,15},{10,... | collective-permute-start | bytes 294920 | tf_op jit(solution)/shard_map/ppermute | solution.py:104
  39.4 6.8 %collective-permute-start.13 = (bf16[12,32,128]{2,1,0:T(8,128)(2,1)S(1)}, bf16[12,32,128]{2,1,0:T(8,128)(2,1)S(1)}, u32[]{:S(2)}, u32[]{:S(2)}) collective-permute-start(bf16[12,32,128]{2,1,0:T(8,128)(2,1)S(1)} %collective-permute-done.9.refs_5_), channel_id=1, source_target_pairs={{0,2},{1,7},{2,4},{3,1},{4,6},{5,3},{6,0},{7,5},{8,10},{9,15},{10,... | collective-permute-start | bytes 294920 | tf_op jit(solution)/shard_map/ppermute | solution.py:104
  50.2 7.0 %collective-permute-start.18 = (bf16[24,32,128]{2,1,0:T(8,128)(2,1)S(1)}, bf16[24,32,128]{2,1,0:T(8,128)(2,1)S(1)}, u32[]{:S(2)}, u32[]{:S(2)}) collective-permute-start(bf16[24,32,128]{2,1,0:T(8,128)(2,1)S(1)} %get-tuple-element.79), channel_id=1, source_target_pairs={{0,1},{1,0},{2,3},{3,2},{4,5},{5,4},{6,7},{7,6},{8,9},{9,8},{10,11... | collective-permute-start | bytes 589832 | tf_op jit(solution)/shard_map/ppermute | solution.py:99
  51.0 8.6 %collective-permute-start.16 = (bf16[24,32,128]{2,1,0:T(8,128)(2,1)S(1)}, bf16[24,32,128]{2,1,0:T(8,128)(2,1)S(1)}, u32[]{:S(2)}, u32[]{:S(2)}) collective-permute-start(bf16[24,32,128]{2,1,0:T(8,128)(2,1)S(1)} %get-tuple-element.73.after_ref), channel_id=1, source_target_pairs={{0,1},{1,0},{2,3},{3,2},{4,5},{5,4},{6,7},{7,6},{8,9},{9,8},{10,11... | collective-permute-start | bytes 589832 | tf_op jit(solution)/shard_map/ppermute | solution.py:99
  52.3 7.3 %collective-permute-start.17 = (s32[49,128]{1,0:T(8,128)S(1)}, s32[49,128]{1,0:T(8,128)S(1)}, u32[]{:S(2)}, u32[]{:S(2)}) collective-permute-start(s32[49,128]{1,0:T(8,128)S(1)} %get-tuple-element.74), channel_id=1, source_target_pairs={{0,1},{1,0},{2,3},{3,2},{4,5},{5,4},{6,7},{7,6},{8,9},{9,8},{10,11... | collective-permute-start | bytes 75272 | tf_op jit(solution)/shard_map/ppermute | solution.py:99
  66.1 7.5 %collective-permute-start.23 = (bf16[12,32,128]{2,1,0:T(8,128)(2,1)S(1)}, bf16[12,32,128]{2,1,0:T(8,128)(2,1)S(1)}, u32[]{:S(2)}, u32[]{:S(2)}) collective-permute-start(bf16[12,32,128]{2,1,0:T(8,128)(2,1)S(1)} %get-tuple-element.85.b_ref), channel_id=1, source_target_pairs={{0,1},{1,2},{2,3},{3,4},{4,5},{5,6},{6,7},{7,0},{8,9},{9,10},{10,1... | collective-permute-start | bytes 294920 | tf_op jit(solution)/shard_map/ppermute | solution.py:94
  66.6 7.0 %collective-permute-start.22 = (bf16[12,32,128]{2,1,0:T(8,128)(2,1)S(1)}, bf16[12,32,128]{2,1,0:T(8,128)(2,1)S(1)}, u32[]{:S(2)}, u32[]{:S(2)}) collective-permute-start(bf16[12,32,128]{2,1,0:T(8,128)(2,1)S(1)} %get-tuple-element.85.b_ref), channel_id=1, source_target_pairs={{1,0},{2,1},{3,2},{4,3},{5,4},{6,5},{7,6},{0,7},{9,8},{10,9},{11,1... | collective-permute-start | bytes 294920 | tf_op jit(solution)/shard_map/ppermute | solution.py:94
  74.8 7.5 %collective-permute-start.25 = (bf16[12,32,128]{2,1,0:T(8,128)(2,1)S(1)}, bf16[12,32,128]{2,1,0:T(8,128)(2,1)S(1)}, u32[]{:S(2)}, u32[]{:S(2)}) collective-permute-start(bf16[12,32,128]{2,1,0:T(8,128)(2,1)S(1)} %get-tuple-element.88.b_ref), channel_id=1, source_target_pairs={{0,1},{1,2},{2,3},{3,4},{4,5},{5,6},{6,7},{7,0},{8,9},{9,10},{10,1... | collective-permute-start | bytes 294920 | tf_op jit(solution)/shard_map/ppermute | solution.py:94
  79.6 7.6 %collective-permute-start.29 = (s32[49,128]{1,0:T(8,128)S(1)}, s32[49,128]{1,0:T(8,128)S(1)}, u32[]{:S(2)}, u32[]{:S(2)}) collective-permute-start(s32[49,128]{1,0:T(8,128)S(1)} %collective-permute-done.17.near_to_ref.near_ref), channel_id=1, source_target_pairs={{0,2},{1,7},{2,4},{3,1},{4,6},{5,3},{6,0},{7,5},{8,10},{9,15},{10,... | collective-permute-start | bytes 75272 | tf_op jit(solution)/shard_map/ppermute | solution.py:104
  104.2 6.6 %collective-permute-start.35 = (bf16[12,8,128]{2,1,0:T(8,128)(2,1)S(1)}, bf16[12,8,128]{2,1,0:T(8,128)(2,1)S(1)}, u32[]{:S(2)}, u32[]{:S(2)}) collective-permute-start(bf16[12,8,128]{2,1,0:T(8,128)(2,1)S(1)} %get-tuple-element.104.x_ref.b_ref), channel_id=1, source_target_pairs={{0,1},{1,2},{2,3},{3,4},{4,5},{5,6},{6,7},{7,0},{8,9},{9,10},{10,1... | collective-permute-start | bytes 73736 | tf_op jit(solution)/shard_map/ppermute | solution.py:94
  104.2 6.6 %collective-permute-start.34 = (bf16[12,8,128]{2,1,0:T(8,128)(2,1)S(1)}, bf16[12,8,128]{2,1,0:T(8,128)(2,1)S(1)}, u32[]{:S(2)}, u32[]{:S(2)}) collective-permute-start(bf16[12,8,128]{2,1,0:T(8,128)(2,1)S(1)} %get-tuple-element.104.x_ref.b_ref), channel_id=1, source_target_pairs={{1,0},{2,1},{3,2},{4,3},{5,4},{6,5},{7,6},{0,7},{9,8},{10,9},{11,1... | collective-permute-start | bytes 73736 | tf_op jit(solution)/shard_map/ppermute | solution.py:94
  111.8 6.6 %collective-permute-start.37 = (bf16[12,8,128]{2,1,0:T(8,128)(2,1)S(1)}, bf16[12,8,128]{2,1,0:T(8,128)(2,1)S(1)}, u32[]{:S(2)}, u32[]{:S(2)}) collective-permute-start(bf16[12,8,128]{2,1,0:T(8,128)(2,1)S(1)} %get-tuple-element.106.x_ref.b_ref), channel_id=1, source_target_pairs={{0,1},{1,2},{2,3},{3,4},{4,5},{5,6},{6,7},{7,0},{8,9},{9,10},{10,1... | collective-permute-start | bytes 73736 | tf_op jit(solution)/shard_map/ppermute | solution.py:94
  111.8 6.6 %collective-permute-start.36 = (bf16[12,8,128]{2,1,0:T(8,128)(2,1)S(1)}, bf16[12,8,128]{2,1,0:T(8,128)(2,1)S(1)}, u32[]{:S(2)}, u32[]{:S(2)}) collective-permute-start(bf16[12,8,128]{2,1,0:T(8,128)(2,1)S(1)} %get-tuple-element.106.x_ref.b_ref), channel_id=1, source_target_pairs={{1,0},{2,1},{3,2},{4,3},{5,4},{6,5},{7,6},{0,7},{9,8},{10,9},{11,1... | collective-permute-start | bytes 73736 | tf_op jit(solution)/shard_map/ppermute | solution.py:94
  119.5 6.6 %collective-permute-start.39 = (bf16[12,8,128]{2,1,0:T(8,128)(2,1)S(1)}, bf16[12,8,128]{2,1,0:T(8,128)(2,1)S(1)}, u32[]{:S(2)}, u32[]{:S(2)}) collective-permute-start(bf16[12,8,128]{2,1,0:T(8,128)(2,1)S(1)} %get-tuple-element.108.x_ref.b_ref), channel_id=1, source_target_pairs={{0,1},{1,2},{2,3},{3,4},{4,5},{5,6},{6,7},{7,0},{8,9},{9,10},{10,1... | collective-permute-start | bytes 73736 | tf_op jit(solution)/shard_map/ppermute | solution.py:94
  127.1 6.6 %collective-permute-start.41 = (bf16[12,8,128]{2,1,0:T(8,128)(2,1)S(1)}, bf16[12,8,128]{2,1,0:T(8,128)(2,1)S(1)}, u32[]{:S(2)}, u32[]{:S(2)}) collective-permute-start(bf16[12,8,128]{2,1,0:T(8,128)(2,1)S(1)} %get-tuple-element.110.x_ref.b_ref), channel_id=1, source_target_pairs={{0,1},{1,2},{2,3},{3,4},{4,5},{5,6},{6,7},{7,0},{8,9},{9,10},{10,1... | collective-permute-start | bytes 73736 | tf_op jit(solution)/shard_map/ppermute | solution.py:94
  127.2 6.6 %collective-permute-start.40 = (bf16[12,8,128]{2,1,0:T(8,128)(2,1)S(1)}, bf16[12,8,128]{2,1,0:T(8,128)(2,1)S(1)}, u32[]{:S(2)}, u32[]{:S(2)}) collective-permute-start(bf16[12,8,128]{2,1,0:T(8,128)(2,1)S(1)} %get-tuple-element.110.x_ref.b_ref), channel_id=1, source_target_pairs={{1,0},{2,1},{3,2},{4,3},{5,4},{6,5},{7,6},{0,7},{9,8},{10,9},{11,1... | collective-permute-start | bytes 73736 | tf_op jit(solution)/shard_map/ppermute | solution.py:94
  134.8 6.8 %collective-permute-start.43 = (bf16[12,8,128]{2,1,0:T(8,128)(2,1)S(1)}, bf16[12,8,128]{2,1,0:T(8,128)(2,1)S(1)}, u32[]{:S(2)}, u32[]{:S(2)}) collective-permute-start(bf16[12,8,128]{2,1,0:T(8,128)(2,1)S(1)} %get-tuple-element.112.x_ref.b_ref), channel_id=1, source_target_pairs={{0,1},{1,2},{2,3},{3,4},{4,5},{5,6},{6,7},{7,0},{8,9},{9,10},{10,1... | collective-permute-start | bytes 73736 | tf_op jit(solution)/shard_map/ppermute | solution.py:94
  147.9 7.4 %collective-permute-start.48 = (bf16[12,32,128]{2,1,0:T(8,128)(2,1)S(1)}, bf16[12,32,128]{2,1,0:T(8,128)(2,1)S(1)}, u32[]{:S(2)}, u32[]{:S(2)}) collective-permute-start(bf16[12,32,128]{2,1,0:T(8,128)(2,1)S(1)} %get-tuple-element.115.b_ref), channel_id=1, source_target_pairs={{0,1},{1,2},{2,3},{3,4},{4,5},{5,6},{6,7},{7,0},{8,9},{9,10},{10,1... | collective-permute-start | bytes 294920 | tf_op jit(solution)/shard_map/ppermute | solution.py:94
  147.9 7.4 %collective-permute-start.47 = (bf16[12,32,128]{2,1,0:T(8,128)(2,1)S(1)}, bf16[12,32,128]{2,1,0:T(8,128)(2,1)S(1)}, u32[]{:S(2)}, u32[]{:S(2)}) collective-permute-start(bf16[12,32,128]{2,1,0:T(8,128)(2,1)S(1)} %get-tuple-element.115.b_ref), channel_id=1, source_target_pairs={{1,0},{2,1},{3,2},{4,3},{5,4},{6,5},{7,6},{0,7},{9,8},{10,9},{11,1... | collective-permute-start | bytes 294920 | tf_op jit(solution)/shard_map/ppermute | solution.py:94
  156.5 6.8 %collective-permute-start.53 = (bf16[12,32,128]{2,1,0:T(8,128)(2,1)S(1)}, bf16[12,32,128]{2,1,0:T(8,128)(2,1)S(1)}, u32[]{:S(2)}, u32[]{:S(2)}) collective-permute-start(bf16[12,32,128]{2,1,0:T(8,128)(2,1)S(1)} %get-tuple-element.117.refs_7_), channel_id=1, source_target_pairs={{0,2},{1,3},{2,4},{3,5},{4,6},{5,7},{6,0},{7,1},{8,10},{9,11},{10,... | collective-permute-start | bytes 294920 | tf_op jit(solution)/shard_map/ppermute | solution.py:668
  156.5 8.9 %collective-permute-start.51 = (bf16[12,32,128]{2,1,0:T(8,128)(2,1)S(1)}, bf16[12,32,128]{2,1,0:T(8,128)(2,1)S(1)}, u32[]{:S(2)}, u32[]{:S(2)}) collective-permute-start(bf16[12,32,128]{2,1,0:T(8,128)(2,1)S(1)} %get-tuple-element.117.refs_7_), channel_id=1, source_target_pairs={{0,4},{1,5},{2,6},{3,7},{4,0},{5,1},{6,2},{7,3},{8,12},{9,13},{10,... | collective-permute-start | bytes 294920 | tf_op jit(solution)/shard_map/ppermute | solution.py:668
  159.7 8.3 %collective-permute-start.49 = (bf16[12,32,128]{2,1,0:T(8,128)(2,1)S(1)}, bf16[12,32,128]{2,1,0:T(8,128)(2,1)S(1)}, u32[]{:S(2)}, u32[]{:S(2)}) collective-permute-start(bf16[12,32,128]{2,1,0:T(8,128)(2,1)S(1)} %get-tuple-element.117.refs_7_), channel_id=1, source_target_pairs={{0,6},{1,7},{2,0},{3,1},{4,2},{5,3},{6,4},{7,5},{8,14},{9,15},{10,... | collective-permute-start | bytes 294920 | tf_op jit(solution)/shard_map/ppermute | solution.py:668
  160.3 7.7 %collective-permute-start.55 = (bf16[12,32,128]{2,1,0:T(8,128)(2,1)S(1)}, bf16[12,32,128]{2,1,0:T(8,128)(2,1)S(1)}, u32[]{:S(2)}, u32[]{:S(2)}) collective-permute-start(bf16[12,32,128]{2,1,0:T(8,128)(2,1)S(1)} %get-tuple-element.117.refs_7_), channel_id=1, source_target_pairs={{0,1},{1,0},{2,3},{3,2},{4,5},{5,4},{6,7},{7,6},{8,9},{9,8},{10,11... | collective-permute-start | bytes 294920 | tf_op jit(solution)/shard_map/ppermute | solution.py:99
  (40 other events, 272.7 us)
